TPU v7x, 256 devices: a whole 4x4x8 slice. The times are simulated.
256 devices in a mesh: blocks: 64 (over z, y, core), obj: 4 (over x).
Axes of the slice: x: 4, y: 4, z: 8, core: 2. Of those that a mesh axis runs over, the one named last changes fastest.
Arguments:
- start_adjoint: float32 [4, 5, 4096, 128], P('obj', None, 'blocks'), may hold values from -6 to 6
- adjoint_source: float32 [4, 5, 4096, 128], P('obj', None, 'blocks'), may hold values from -6 to 6
- block_inverse: float32 [5, 5, 4096, 128], P(None, None, 'blocks'), may hold values from -0.12 to 0.8
- coupling: float32 [4, 4096, 128], P(None, 'blocks'), may hold values from 0.02 to 0.15
- send_cell: int32 [262144], P('blocks'), may hold values from 0 to 8191
- face_peer: int32 [262144, 1], P('blocks'), may hold values from 0 to 63; in each aligned block of 4096 rows (0 to 4095, 4096 to 8191, ...) at most 128 rows name the same one
- receive_cell: int32 [262144], P('blocks'), may hold values from 0 to 8191
- face_weight: float32 [262144], P('blocks'), may hold values from 0.05 to 0.3
- surface_cell: int32 [524288], P('blocks'), may hold values from 0 to 8191
- surface_grad: float32 [3, 5, 524288], P(None, None, 'blocks'), may hold values from -6 to 6
- objective_weight: float32 [4], replicated, may hold values from 0.25 to 1
- deform_owner: int32 [524288, 1], P(('blocks', 'obj')), may hold values from 0 to 63; in each aligned block of 2048 rows (0 to 2047, 2048 to 4095, ...) at most 64 rows name the same one
- deform_node: int32 [524288], P(('blocks', 'obj')), may hold values from 0 to 16383
- mesh_start: float32 [3, 256, 128, 128], P(None, 'blocks', 'obj'), may hold values from -6 to 6
- stiffness: float32 [256, 128, 128], P('blocks', 'obj'), may hold values from 0.1 to 2
Outputs:
- flow_adjoint: float32 [4, 5, 4096, 128], P('obj', None, 'blocks')
- mesh_adjoint: float32 [3, 256, 128, 128], P(None, 'blocks', 'obj')
Inputs may be any that keep to these rules, and one draw needn't show every extreme that they name: `face_peer`: among the 4096 rows of one index of blocks no block is named more than 128 times, and this bound is reached. `deform_owner`: among the 2048 rows of one device no block is named more than 64 times, and this bound is reached.
All inputs are finite; a program needn't handle non-finite values.
Results may differ from a plain program's by a relative error of at most 0.0001.
Values sent between devices are 32-bit elements; how exact they have to be, the bound alone decides.
A program may use at most 192 MiB of HBM per device.

v0:
```python
import jax
import jax.numpy as jnp
from jax import lax
from jax.sharding import PartitionSpec as P

FLOW_SWEEPS = 3
DEF_SWEEPS = 2


OMEGA = 0.8


def extended(cells, sides, width):
    for axis, dim in sides:
        count = lax.axis_size(axis)
        ends = count - 1
        head = lax.slice_in_dim(cells, 0, width, axis=dim)
        tail = lax.slice_in_dim(cells, cells.shape[dim] - width, cells.shape[dim], axis=dim)
        cells = jnp.concatenate(
            [
                lax.ppermute(tail, axis, [(i, (i + 1) % count) for i in range(ends)]),
                cells,
                lax.ppermute(head, axis, [((i + 1) % count, i) for i in range(ends)]),
            ],
            axis=dim,
        )
    return cells


def bucket_slots(destination, peer_count, capacity):
    peer_ids = jnp.arange(peer_count, dtype=jnp.int32)
    onehot = (destination[None, :] == peer_ids[:, None]).astype(jnp.int32)
    ranking = jnp.cumsum(onehot, axis=1) - 1
    within = jnp.sum(onehot * ranking, axis=0)
    return destination * capacity + within


def interior_terms(adjoint, couple_coef):
    zero_rows = jnp.zeros_like(adjoint[:, :1, :])
    below = jnp.concatenate([zero_rows, adjoint[:, :-1, :]], axis=1)
    above = jnp.concatenate([adjoint[:, 1:, :], zero_rows], axis=1)
    zero_cols = jnp.zeros_like(adjoint[:, :, :1])
    left_side = jnp.concatenate([zero_cols, adjoint[:, :, :-1]], axis=2)
    right_side = jnp.concatenate([adjoint[:, :, 1:], zero_cols], axis=2)
    return (
        couple_coef[0] * below
        + couple_coef[1] * above
        + couple_coef[2] * left_side
        + couple_coef[3] * right_side
    )


def block_product(matrix, vector):
    stacked_rows = []
    for row_idx in range(matrix.shape[0]):
        accum_sum = matrix[row_idx, 0] * vector[0]
        for col_idx in range(1, matrix.shape[1]):
            accum_sum = accum_sum + matrix[row_idx, col_idx] * vector[col_idx]
        stacked_rows.append(accum_sum)
    return jnp.stack(stacked_rows, axis=0)


def relax(wider, surface_force, stiff_part):
    center = wider[:, 1:-1, 1:-1, :]
    zero_cols = jnp.zeros_like(center[..., :1])
    beside = wider[:, 2:, 1:-1, :] + wider[:, :-2, 1:-1, :]
    beside = beside + wider[:, 1:-1, 2:, :] + wider[:, 1:-1, :-2, :]
    beside = (
        beside
        + jnp.concatenate([center[..., 1:], zero_cols], axis=3)
        + jnp.concatenate([zero_cols, center[..., :-1]], axis=3)
    )
    return (1.0 - OMEGA) * center + OMEGA * (surface_force + beside) / (6.0 + stiff_part)


def shards(
    start_adjoint,
    adjoint_source,
    block_inverse,
    coupling,
    send_cell,
    face_peer,
    receive_cell,
    face_weight,
    surface_cell,
    surface_grad,
    objective_weight,
    deform_owner,
    deform_node,
    mesh_start,
    stiffness,
):
    block_count = lax.axis_size("blocks")
    face_count = send_cell.shape[0]
    face_cap = 2 * face_count // block_count
    fields = start_adjoint.shape[1]
    rows_y = start_adjoint.shape[2]
    cols_z = start_adjoint.shape[3]
    cell_count = rows_y * cols_z
    adjoint = start_adjoint[0]
    source_term = adjoint_source[0]
    block_inv = block_inverse.reshape(fields, fields, cell_count)
    face_slot = bucket_slots(face_peer[:, 0], block_count, face_cap)
    target_send = (
        jnp.zeros((block_count * face_cap,), jnp.int32)
        .at[face_slot]
        .set(receive_cell)
        .reshape(block_count, face_cap)
    )
    target_cell = lax.all_to_all(
        target_send, "blocks", split_axis=0, concat_axis=0, tiled=True
    ).reshape(-1)
    for sweep_idx in range(FLOW_SWEEPS):
        flat_cells = adjoint.reshape(fields, cell_count)
        outgoing = flat_cells[:, send_cell] * face_weight[None, :]
        packed = (
            jnp.zeros((fields, block_count * face_cap), jnp.float32)
            .at[:, face_slot]
            .set(outgoing)
            .reshape(fields, block_count, face_cap)
        )
        arrived = lax.all_to_all(packed, "blocks", split_axis=1, concat_axis=1, tiled=True).reshape(
            fields, block_count * face_cap
        )
        local_term = (source_term + interior_terms(adjoint, coupling)).reshape(fields, cell_count)
        face_terms = jnp.zeros((fields, cell_count), jnp.float32).at[:, target_cell].add(arrived)
        updated = (1.0 - OMEGA) * flat_cells + OMEGA * block_product(
            block_inv, local_term + face_terms
        )
        adjoint = updated.reshape(fields, rows_y, cols_z)
    flat_cells = adjoint.reshape(fields, cell_count)
    surface_values = flat_cells[:, surface_cell]
    obj_index = lax.axis_index("obj")
    obj_count = lax.axis_size("obj")
    surf_count = surface_cell.shape[0]
    quarter = surf_count // obj_count
    comps = surface_grad.shape[0]
    weight_here = objective_weight[obj_index]
    weighted_term = weight_here * jnp.sum(surface_grad * surface_values[None], axis=1)
    combined = lax.psum_scatter(weighted_term, "obj", scatter_dimension=1, tiled=True)
    relay_cap = 2 * quarter // block_count
    relay_slot = bucket_slots(deform_owner[:, 0], block_count, relay_cap)
    value_pack = (
        jnp.zeros((comps, block_count * relay_cap), jnp.float32)
        .at[:, relay_slot]
        .set(combined)
        .reshape(comps, block_count, relay_cap)
    )
    index_pack = (
        jnp.zeros((1, block_count * relay_cap), jnp.int32)
        .at[:, relay_slot]
        .set(deform_node[None, :])
        .reshape(1, block_count, relay_cap)
    )
    got_values, got_index = (
        lax.all_to_all(value_pack, "blocks", split_axis=1, concat_axis=1, tiled=True),
        lax.all_to_all(index_pack, "blocks", split_axis=1, concat_axis=1, tiled=True),
    )
    size_x = mesh_start.shape[1]
    size_y = mesh_start.shape[2]
    size_z = mesh_start.shape[3]
    node_count = size_x * size_y * size_z
    surface_force = (
        jnp.zeros((comps, node_count), jnp.float32)
        .at[:, got_index.reshape(-1)]
        .add(got_values.reshape(comps, -1))
        .reshape(comps, size_x, size_y, size_z)
    )
    mesh_field = mesh_start
    for sweep_idx in range(DEF_SWEEPS):
        padded = extended(mesh_field, (("blocks", 1), ("obj", 2)), 1)
        mesh_field = relax(padded, surface_force, stiffness)
    return (adjoint[None], mesh_field)


def solution(mesh):
    placed = (
        P("obj", None, "blocks", None),
        P("obj", None, "blocks", None),
        P(None, None, "blocks", None),
        P(None, "blocks", None),
        P("blocks"),
        P("blocks", None),
        P("blocks"),
        P("blocks"),
        P("blocks"),
        P(None, None, "blocks"),
        P(),
        P(("blocks", "obj"), None),
        P(("blocks", "obj")),
        P(None, "blocks", "obj", None),
        P("blocks", "obj", None),
    )
    return jax.shard_map(
        shards,
        mesh=mesh,
        in_specs=placed,
        out_specs=(P("obj", None, "blocks", None), P(None, "blocks", "obj", None)),
        check_vma=False,
    )
```

profile of v0, /device:TPU:1, one launch (start us, length us, event | category | flops | bytes accessed | tf_op | source)
XLA Modules:
  0.0 769.6 jit_solution(1421126083909200900)
XLA Ops:
  8.0 18.1 %reduce-window.16 = s32[64,16,128]{2,1,0:T(8,128)S(1)} reduce-window(s32[64,16,128]{2,1,0:T(8,128)S(1)} %fusion.17, s32[]{:T(128)} %constant.15.clone.1), window={size=1x1x128 pad=0_0x0_0x127_0}, to_apply=%region_10.11 | reduce-window | flops 16646144 | bytes 1048580 | tf_op jit(solution)/shard_map/reduce-window.2
  37.6 13.3 %all-to-all-start.4 = ((s32[1,64,64]{2,0,1:T(1,128)}), s32[1,64,64]{2,0,1:T(1,128)}, u32[]{:S(2)}, u32[]{:S(2)}) async-start(s32[1,64,64]{2,0,1:T(1,128)} %reshape.485), calls=%async_computation.4 | async-start | bytes 65536 | tf_op jit(solution)/shard_map/all_to_all | solution.py:157
  59.0 18.4 %reduce-window.14 = s32[64,32,128]{2,1,0:T(8,128)S(1)} reduce-window(s32[64,32,128]{2,1,0:T(8,128)S(1)} %fusion.16, s32[]{:T(128)} %constant.15.clone.1), window={size=1x1x128 pad=0_0x0_0x127_0}, to_apply=%region_0.0 | reduce-window | flops 33292288 | bytes 2097156 | tf_op jit(solution)/shard_map/reduce-window
  89.8 37.8 %scatter_custom_fusion.1 = f32[5,8192]{0,1:T(8,128)} fusion(s32[4096]{0:T(1024)S(1)} %bitcast.350, f32[]{:T(128)} %constant.14.clone.1, f32[4096]{0:T(1024)S(1)} %copy-done.31, f32[5,8192]{0,1:T(8,128)} %copy.462, s32[4096]{0:T(1024)S(1)} %fusion.37), kind=kCustom, calls=%fused_computation.20 | custom fusion | flops 20480 | bytes 360452 | tf_op jit(solution)/shard_map/scatter | solution.py:119
  131.1 16.3 %scatter_custom_fusion = s32[8192]{0:T(1024)} fusion(s32[4096]{0:T(1024)S(1)} %bitcast.351, s32[4096]{0:T(1024)} %param.21, s32[]{:T(128)} %constant.15.clone.1), kind=kCustom, calls=%fused_computation.159 | custom fusion | bytes 33280 | tf_op jit(solution)/shard_map/scatter | solution.py:107
  148.2 11.3 %all-to-all-start = ((s32[64,1,128]{2,1,0:T(1,128)}), s32[64,1,128]{2,1,0:T(1,128)S(1)}, u32[]{:S(2)}, u32[]{:S(2)}) async-start(s32[64,1,128]{2,1,0:T(1,128)} %bitcast.15), calls=%async_computation | async-start | bytes 65536 | tf_op jit(solution)/shard_map/all_to_all | solution.py:110
  170.4 11.2 %all-to-all-start.1 = ((f32[5,64,128]{2,0,1:T(8,128)}), f32[5,64,128]{2,0,1:T(8,128)S(1)}, u32[]{:S(2)}, u32[]{:S(2)}) async-start(f32[5,64,128]{2,0,1:T(8,128)} %copy.463), calls=%async_computation.1 | async-start | bytes 524288 | tf_op jit(solution)/shard_map/all_to_all | solution.py:122
  181.6 13.1 %all-to-all-done.1 = f32[5,64,128]{2,0,1:T(8,128)S(1)} async-done(((f32[5,64,128]{2,0,1:T(8,128)}), f32[5,64,128]{2,0,1:T(8,128)S(1)}, u32[]{:S(2)}, u32[]{:S(2)}) %all-to-all-start.1) | async-done | bytes 163872 | tf_op jit(solution)/shard_map/all_to_all | solution.py:122
  197.5 51.3 %scatter_fusion = f32[5,8192]{0,1:T(8,128)} fusion(f32[5,8192]{0,1:T(8,128)} %bitcast.291, s32[8192]{0:T(1024)S(1)} %bitcast.308, f32[8192,5]{1,0:T(8,128)} %copy.464), kind=kCustom, calls=%fused_computation.6 | custom fusion | flops 40960 | bytes 524288 | tf_op jit(solution)/shard_map/scatter-add | solution.py:126
  248.8 16.8 %fusion.47 = (f32[1,8192]{0,1:T(8,128)}, f32[1,8192]{0,1:T(8,128)}, f32[1,8192]{0,1:T(8,128)}, f32[1,8192]{0,1:T(8,128)}, f32[1,8192]{0,1:T(8,128)}) fusion(f32[5,8192]{0,1:T(8,128)} %scatter_fusion), kind=kLoop, calls=%fused_computation.171 | loop fusion | bytes 327680 | tf_op jit(solution)/shard_map/slice | solution.py:56
  285.5 37.7 %scatter_custom_fusion.3 = f32[5,8192]{0,1:T(8,128)} fusion(s32[4096]{0:T(1024)S(1)} %bitcast.352, f32[]{:T(128)} %constant.14.clone.1, f32[4096]{0:T(1024)S(1)} %copy-done.31, f32[5,8192]{0,1:T(8,128)} %copy.471, s32[4096]{0:T(1024)S(1)} %fusion.37), kind=kCustom, calls=%fused_computation.18 | custom fusion | flops 20480 | bytes 360452 | tf_op jit(solution)/shard_map/scatter | solution.py:119
  326.8 9.0 %all-to-all-start.2 = ((f32[5,64,128]{2,0,1:T(8,128)}), f32[5,64,128]{2,0,1:T(8,128)S(1)}, u32[]{:S(2)}, u32[]{:S(2)}) async-start(f32[5,64,128]{2,0,1:T(8,128)} %copy.472), calls=%async_computation.2 | async-start | bytes 524288 | tf_op jit(solution)/shard_map/all_to_all | solution.py:122
  340.5 8.3 %all-to-all-done.2 = f32[5,64,128]{2,0,1:T(8,128)S(1)} async-done(((f32[5,64,128]{2,0,1:T(8,128)}), f32[5,64,128]{2,0,1:T(8,128)S(1)}, u32[]{:S(2)}, u32[]{:S(2)}) %all-to-all-start.2) | async-done | bytes 163872 | tf_op jit(solution)/shard_map/all_to_all | solution.py:122
  351.5 51.3 %scatter_fusion.1 = f32[5,8192]{0,1:T(8,128)} fusion(f32[5,8192]{0,1:T(8,128)} %bitcast.293, s32[8192]{0:T(1024)S(1)} %bitcast.309, f32[8192,5]{1,0:T(8,128)} %copy.473), kind=kCustom, calls=%fused_computation.8 | custom fusion | flops 40960 | bytes 524288 | tf_op jit(solution)/shard_map/scatter-add | solution.py:126
  402.9 16.9 %fusion.46 = (f32[1,8192]{0,1:T(8,128)}, f32[1,8192]{0,1:T(8,128)}, f32[1,8192]{0,1:T(8,128)}, f32[1,8192]{0,1:T(8,128)}, f32[1,8192]{0,1:T(8,128)}) fusion(f32[5,8192]{0,1:T(8,128)} %scatter_fusion.1), kind=kLoop, calls=%fused_computation.170 | loop fusion | bytes 327680 | tf_op jit(solution)/shard_map/slice | solution.py:56
  439.0 38.0 %scatter_custom_fusion.5 = f32[5,8192]{0,1:T(8,128)} fusion(s32[4096]{0:T(1024)} %bitcast.353, f32[]{:T(128)} %constant.14.clone.1, f32[4096]{0:T(1024)S(1)} %copy-done.32, f32[5,8192]{0,1:T(8,128)} %copy.480, s32[4096]{0:T(1024)S(1)} %fusion.37), kind=kCustom, calls=%fused_computation.16 | custom fusion | flops 20480 | bytes 4391424 | tf_op jit(solution)/shard_map/scatter | solution.py:119
  480.6 8.8 %all-to-all-start.3 = ((f32[5,64,128]{2,0,1:T(8,128)}), f32[5,64,128]{2,0,1:T(8,128)S(1)}, u32[]{:S(2)}, u32[]{:S(2)}) async-start(f32[5,64,128]{2,0,1:T(8,128)} %copy.481), calls=%async_computation.3 | async-start | bytes 524288 | tf_op jit(solution)/shard_map/all_to_all | solution.py:122
  505.3 51.3 %scatter_fusion.2 = f32[5,8192]{0,1:T(8,128)} fusion(f32[5,8192]{0,1:T(8,128)} %bitcast.292, s32[8192]{0:T(1024)S(1)} %bitcast.310, f32[8192,5]{1,0:T(8,128)} %copy.482), kind=kCustom, calls=%fused_computation.10 | custom fusion | flops 40960 | bytes 524288 | tf_op jit(solution)/shard_map/scatter-add | solution.py:126
  556.6 16.9 %fusion.45 = (f32[1,8192]{0,1:T(8,128)}, f32[1,8192]{0,1:T(8,128)}, f32[1,8192]{0,1:T(8,128)}, f32[1,8192]{0,1:T(8,128)}, f32[1,8192]{0,1:T(8,128)}) fusion(f32[5,8192]{0,1:T(8,128)} %scatter_fusion.2), kind=kLoop, calls=%fused_computation.169 | loop fusion | bytes 327680 | tf_op jit(solution)/shard_map/slice | solution.py:56
  591.5 29.9 %gather_fusion = f32[8192,5]{1,0:T(8,128)} fusion(f32[5,8192]{0,1:T(8,128)} %copy.490, s32[8192]{0:T(1024)S(1)} %copy-done.34), kind=kCustom, calls=%fused_computation.3 | custom fusion | bytes 360448 | tf_op jit(solution)/shard_map/gather | solution.py:132
  627.8 48.8 %reduce-scatter.4.cloned.1.call-done = f32[2048,3]{1,0:T(8,128)} async-done(((f32[8192,3]{1,0:T(8,128)}), f32[2048,3]{1,0:T(8,128)}) %reduce-scatter.4.cloned.1.call-update) | async-done | bytes 24592
  688.7 11.0 %all-to-all-start.5 = ((f32[64,1,192]{2,1,0:T(1,128)}), f32[64,1,192]{2,1,0:T(1,128)S(1)}, u32[]{:S(2)}, u32[]{:S(2)}) async-start(f32[64,1,192]{2,1,0:T(1,128)} %reshape.659), calls=%async_computation.5 | async-start | bytes 131072 | tf_op jit(solution)/shard_map/all_to_all | solution.py:156
  699.7 9.9 %all-to-all-done.5 = f32[64,1,192]{2,1,0:T(1,128)S(1)} async-done(((f32[64,1,192]{2,1,0:T(1,128)}), f32[64,1,192]{2,1,0:T(1,128)S(1)}, u32[]{:S(2)}, u32[]{:S(2)}) %all-to-all-start.5) | async-done | bytes 49184 | tf_op jit(solution)/shard_map/all_to_all | solution.py:156
  713.3 29.1 %scatter_custom_fusion.9 = f32[3,16384]{0,1:T(8,128)} fusion(s32[4096]{0:T(1024)} %bitcast.354, f32[4096,3]{1,0:T(8,128)} %copy.495, f32[]{:T(128)} %constant.14.clone.1), kind=kCustom, calls=%fused_computation.14 | custom fusion | flops 12288 | bytes 197120 | tf_op jit(solution)/shard_map/scatter-add | solution.py:166
  (231 shorter events, 179.2 us)
Async XLA Ops:
  7.2 51.5 %copy-start.1 = (f32[3,4,32,128]{3,2,1,0:T(8,128)S(1)}, f32[3,4,32,128]{3,2,1,0:T(8,128)}, u32[]{:S(2)}) copy-start(f32[3,4,32,128]{3,2,1,0:T(8,128)} %param.28) | copy-start | bytes 589828
  7.2 50.7 %copy-start = (f32[1,5,64,128]{3,2,1,0:T(8,128)S(1)}, f32[1,5,64,128]{3,2,1,0:T(8,128)}, u32[]{:S(2)}) copy-start(f32[1,5,64,128]{3,2,1,0:T(8,128)} %param.15) | copy-start | bytes 491524
  7.2 51.6 %copy-start.35 = (f32[4,64,128]{2,1,0:T(8,128)S(1)}, f32[4,64,128]{2,1,0:T(8,128)}, u32[]{:S(2)}) copy-start(f32[4,64,128]{2,1,0:T(8,128)} %param.18) | copy-start | bytes 393220
  7.2 51.7 %copy-start.33 = (s32[4096,1]{0,1:T(1,128)S(1)}, s32[4096,1]{0,1:T(1,128)}, u32[]{:S(2)}) copy-start(s32[4096,1]{0,1:T(1,128)} %param.20) | copy-start | bytes 49156
  37.6 110.6 %all-to-all-start.4 = ((s32[1,64,64]{2,0,1:T(1,128)}), s32[1,64,64]{2,0,1:T(1,128)}, u32[]{:S(2)}, u32[]{:S(2)}) async-start(s32[1,64,64]{2,0,1:T(1,128)} %reshape.485), calls=%async_computation.4 | async-start | bytes 65536 | tf_op jit(solution)/shard_map/all_to_all | solution.py:157
  52.4 109.8 %collective-permute-start.1 = (f32[3,1,32,128]{3,2,1,0:T(8,128)}, f32[3,1,32,128]{3,2,1,0:T(8,128)}, u32[]{:S(2)}, u32[]{:S(2)}) collective-permute-start(f32[3,1,32,128]{3,2,1,0:T(8,128)} %get-tuple-element.40), channel_id=1, source_target_pairs={{0,4},{4,8},{8,12},{12,16},{16,20},{20,24},{24,28},{28,32},{32,36}... | collective-permute-start | bytes 147464 | tf_op jit(solution)/shard_map/ppermute | solution.py:21
  55.9 107.1 %collective-permute-start = (f32[3,1,32,128]{3,2,1,0:T(8,128)}, f32[3,1,32,128]{3,2,1,0:T(8,128)}, u32[]{:S(2)}, u32[]{:S(2)}) collective-permute-start(f32[3,1,32,128]{3,2,1,0:T(8,128)} %get-tuple-element.39), channel_id=1, source_target_pairs={{4,0},{8,4},{12,8},{16,12},{20,16},{24,20},{28,24},{32,28},{36,32}... | collective-permute-start | bytes 147464 | tf_op jit(solution)/shard_map/ppermute | solution.py:23
  80.2 205.3 %copy-start.36 = (s32[4096,1]{0,1:T(1,128)}, s32[4096,1]{0,1:T(1,128)S(1)}, u32[]{:S(2)}) copy-start(s32[4096,1]{0,1:T(1,128)S(1)} %compare_select_fusion.2) | copy-start | bytes 49156
  148.2 22.2 %all-to-all-start = ((s32[64,1,128]{2,1,0:T(1,128)}), s32[64,1,128]{2,1,0:T(1,128)S(1)}, u32[]{:S(2)}, u32[]{:S(2)}) async-start(s32[64,1,128]{2,1,0:T(1,128)} %bitcast.15), calls=%async_computation | async-start | bytes 65536 | tf_op jit(solution)/shard_map/all_to_all | solution.py:110
  164.5 583.1 %collective-permute-start.2 = (f32[3,6,1,128]{3,2,1,0:T(1,128)}, f32[3,6,1,128]{3,2,1,0:T(1,128)}, u32[]{:S(2)}, u32[]{:S(2)}) collective-permute-start(f32[3,6,1,128]{3,2,1,0:T(1,128)} %get-tuple-element.31), channel_id=1, source_target_pairs={{1,0},{2,1},{3,2},{5,4},{6,5},{7,6},{9,8},{10,9},{11,10},{13,12},{... | collective-permute-start | bytes 27656 | tf_op jit(solution)/shard_map/ppermute | solution.py:23
  165.8 581.9 %collective-permute-start.3 = (f32[3,6,1,128]{3,2,1,0:T(1,128)}, f32[3,6,1,128]{3,2,1,0:T(1,128)}, u32[]{:S(2)}, u32[]{:S(2)}) collective-permute-start(f32[3,6,1,128]{3,2,1,0:T(1,128)} %get-tuple-element.32), channel_id=1, source_target_pairs={{0,1},{1,2},{2,3},{4,5},{5,6},{6,7},{8,9},{9,10},{10,11},{12,13},{... | collective-permute-start | bytes 27656 | tf_op jit(solution)/shard_map/ppermute | solution.py:21
  170.4 24.4 %all-to-all-start.1 = ((f32[5,64,128]{2,0,1:T(8,128)}), f32[5,64,128]{2,0,1:T(8,128)S(1)}, u32[]{:S(2)}, u32[]{:S(2)}) async-start(f32[5,64,128]{2,0,1:T(8,128)} %copy.463), calls=%async_computation.1 | async-start | bytes 524288 | tf_op jit(solution)/shard_map/all_to_all | solution.py:122
  280.7 42.5 %copy-start.23 = (f32[1,8192]{1,0:T(1,128)}, f32[1,8192]{1,0:T(1,128)S(1)}, u32[]{:S(2)}) copy-start(f32[1,8192]{1,0:T(1,128)S(1)} %multiply_add_fusion.20) | copy-start | bytes 98308
  326.8 22.0 %all-to-all-start.2 = ((f32[5,64,128]{2,0,1:T(8,128)}), f32[5,64,128]{2,0,1:T(8,128)S(1)}, u32[]{:S(2)}, u32[]{:S(2)}) async-start(f32[5,64,128]{2,0,1:T(8,128)} %copy.472), calls=%async_computation.2 | async-start | bytes 524288 | tf_op jit(solution)/shard_map/all_to_all | solution.py:122
  340.4 62.4 %copy-start.27 = (f32[1,5,64,128]{3,2,1,0:T(8,128)}, f32[1,5,64,128]{3,2,1,0:T(8,128)S(1)}, u32[]{:S(2)}) copy-start(f32[1,5,64,128]{3,2,1,0:T(8,128)S(1)} %constant_dynamic-update-slice_fusion.1) | copy-start | bytes 491524
  480.6 22.0 %all-to-all-start.3 = ((f32[5,64,128]{2,0,1:T(8,128)}), f32[5,64,128]{2,0,1:T(8,128)S(1)}, u32[]{:S(2)}, u32[]{:S(2)}) async-start(f32[5,64,128]{2,0,1:T(8,128)} %copy.481), calls=%async_computation.3 | async-start | bytes 524288 | tf_op jit(solution)/shard_map/all_to_all | solution.py:122
  489.4 187.2 %reduce-scatter.4.cloned.1.call-start = ((), (), s32[]{:S(2)}) async-start(), calls=%async_computation.7 | async-start | bytes 5242880
  496.2 60.4 %copy-start.29 = (f32[1,5,64,128]{3,2,1,0:T(8,128)}, f32[1,5,64,128]{3,2,1,0:T(8,128)S(1)}, u32[]{:S(2)}) copy-start(f32[1,5,64,128]{3,2,1,0:T(8,128)S(1)} %get-tuple-element.58) | copy-start | bytes 491524
  591.5 32.8 %copy-start.4 = (f32[3,5,8192]{2,0,1:T(4,128)S(1)}, f32[3,5,8192]{2,0,1:T(4,128)}, u32[]{:S(2)}) copy-start(f32[3,5,8192]{2,0,1:T(4,128)} %param.24) | copy-start | bytes 1474564
  688.7 21.0 %all-to-all-start.5 = ((f32[64,1,192]{2,1,0:T(1,128)}), f32[64,1,192]{2,1,0:T(1,128)S(1)}, u32[]{:S(2)}, u32[]{:S(2)}) async-start(f32[64,1,192]{2,1,0:T(1,128)} %reshape.659), calls=%async_computation.5 | async-start | bytes 131072 | tf_op jit(solution)/shard_map/all_to_all | solution.py:156
  748.7 6.3 collective-permute-start.4
  750.6 4.8 collective-permute-start.5
  755.4 5.4 collective-permute-start.6
  756.7 4.8 collective-permute-start.7
  (30 other events, 331.2 us)
Sparse Core Ops, SparseCore 0:
  627.8 48.7 reduce-scatter.3
where the time goes:
time: 784 us; the launch traced here: 770 us
  other arithmetic  353 us (45%)
  local copies, waits for them, and re-layouts  227 us (29%)
  waiting for transfers between devices  87.7 us (11%)
  starting transfers between devices  86.8 us (11%)
  between operations  15.5 us (2%)
    scatter-add x3, other arithmetic, shards(): jnp.zeros((fields, cell_count), jnp.float32).at[:, target_cell].add(arrived)  154 us
    scatter x3, other arithmetic, shards(): packed = jnp.zeros((fields, block_count * face_cap), jnp.float32).at[:, f...  114 us
    unnamed x120, local copies, waits for them, and re-layouts  51.5 us
    slice x3, local copies, waits for them, and re-layouts, block_product(): accum_sum = matrix[row_idx, 0] * vector[0]  50.5 us
    unnamed x2, waiting for transfers between devices  48.9 us
    another operation x4, other arithmetic  37.7 us
    gather x2, local copies, waits for them, and re-layouts, shards(): surface_values = flat_cells[:, surface_cell]  32.8 us
    scatter-add x1, other arithmetic, shards(): surface_force = jnp.zeros((comps, node_count), jnp.float32).at[:, got_ind...  29.1 us
  transfers between devices with their start and end apart: 15, of which 7 were waited for; matrix products, arithmetic and copies ran while one was open for 71% of the time, Pallas kernels for 0%

commit v1 on v0

v1 whole, which is shorter than its diff:
```python
import functools

import jax
import jax.numpy as jnp
from jax import lax
from jax.experimental import pallas as pl
from jax.experimental.pallas import tpu as pltpu
from jax.sharding import PartitionSpec as P

OMEGA = 0.8
SWEEPS = 3
GROUPS = 4

f32, bf16, i32 = jnp.float32, jnp.bfloat16, jnp.int32
LANES = 128
WIDE = 256


def dot(a, b):
    return lax.dot_general(a, b, (((1,), (0,)), ((), ())), preferred_element_type=f32)


def dot_nt(a, b):
    return lax.dot_general(a, b, (((1,), (1,)), ((), ())), preferred_element_type=f32)


def iota(shape, dim):
    return lax.broadcasted_iota(i32, shape, dim)


def fiota(shape, dim):
    return iota(shape, dim).astype(f32)


def halves(x):
    high = x.astype(bf16).astype(f32)
    return high, x - high


def pair(array, k):
    return jnp.concatenate([array[2 * k : 2 * k + 1], array[2 * k + 1 : 2 * k + 2]], axis=1)


def pair_at(ref, k):
    return jnp.concatenate([ref[pl.ds(2 * k, 1), :], ref[pl.ds(2 * k + 1, 1), :]], axis=1)


def bucket_ranks(bucket, chunks, buckets, lhs):
    before = jnp.zeros((buckets, WIDE), f32)
    ids = iota((buckets, WIDE), 0)
    hots = []
    for g in range(chunks):
        hot = jnp.where(ids == pair(bucket, g), 1.0, 0.0)
        rows = slice(g * buckets, (g + 1) * buckets)
        lhs[rows, 0:WIDE] = hot.astype(bf16)
        lhs[rows, WIDE : 2 * WIDE] = before.astype(bf16)
        before = before + hot
    a, b = iota((2 * WIDE, WIDE), 0), iota((2 * WIDE, WIDE), 1)
    upto = jnp.where((a <= b) | (a >= WIDE), 1.0, 0.0).astype(bf16)
    counts = dot(lhs[0 : chunks * buckets, :], upto)
    ranks = []
    for g in range(chunks):
        hot = jnp.where(ids == pair(bucket, g), 1.0, 0.0)
        ranks.append(jnp.sum(counts[g * buckets : (g + 1) * buckets] * hot, axis=0, keepdims=True) - 1.0)
    return ranks


def slot_maps(row_of, rows, ranks, values, lhs, hot_slot):
    ids = iota((rows, WIDE), 0)
    slots = fiota((LANES, WIDE), 0)
    chunks = len(ranks)
    for g in range(chunks):
        lanes = slice(g * WIDE, (g + 1) * WIDE)
        hot_slot[:, lanes] = jnp.where(slots == ranks[g], 1.0, 0.0).astype(bf16)
        mask = ids == pair(row_of, g)
        for j, value in enumerate(values):
            lhs[j * rows : (j + 1) * rows, lanes] = jnp.where(mask, pair(value, g), 0.0).astype(bf16)
    return dot_nt(lhs[0 : len(values) * rows, 0 : chunks * WIDE], hot_slot[:, 0 : chunks * WIDE])


def shifted(x, shift, axis):
    size = x.shape[axis]
    at = iota(x.shape, axis)
    edge = 0 if shift == 1 else size - 1
    return jnp.where(at == edge, 0.0, pltpu.roll(x, 1 if shift == 1 else size - 1, axis))


def kernel(
    n_blocks, n_obj, fields, rows_y, faces, surf, comps, size_x, size_y,
    start_ref, source_hbm, binv_hbm, coup_hbm, send_ref, peer_ref, recv_ref, wgt_ref, scell_ref, grad_hbm, oweight_ref,
    owner_ref, node_ref, mesh_hbm, stiff_hbm,
    flow_hbm, meshout_hbm,
    source, binv, coup, grad, mesh0, stiff,
    rank_lhs, map_lhs, map_hot, scol_m, srow_m, wgt_m,
    chot, wmask, surf_hot, surf_mask, lam, xhl, local,
    sbuf0, rbuf0, sbuf1, rbuf1, recv_hot, recv_lhs,
    ssend, srecv, comb, vhl,
    rcol_m, rrow_m, relay_hot, relay_mask, isend, irecv, vsend, vrecv, node_hot, node_lhs, inode,
    mesh1, mesh2, base, coef, ysend, yrecv, xrecv,
    in_sem, out_sem, self_sem, send_sem, recv_sem, obj_send, obj_recv, halo_send, halo_recv,
):
    b, o = lax.axis_index("blocks"), lax.axis_index("obj")
    chips = n_blocks // 2
    chip, core = b // 2, b % 2
    half_y = rows_y // 2
    group = chips // GROUPS
    quarter = surf // n_obj
    qrows = quarter // LANES

    barrier = pltpu.get_barrier_semaphore()

    def greet(t, carry):
        pl.semaphore_signal(barrier, inc=1, device_id={"blocks": lax.rem(b + t, n_blocks)})
        return carry

    lax.fori_loop(1, n_blocks, greet, 0)
    for s in range(1, n_obj):
        pl.semaphore_signal(barrier, inc=1, device_id={"obj": lax.rem(o + s, n_obj)})

    loads = []
    for k, (src, dst) in enumerate(
        ((source_hbm, source), (coup_hbm, coup), (binv_hbm, binv), (mesh_hbm, mesh0), (stiff_hbm, stiff), (grad_hbm, grad))
    ):
        copy = pltpu.make_async_copy(src, dst, in_sem.at[k])
        copy.start()
        loads.append(copy)

    peer = peer_ref[...]
    slot_row = (((peer >> 1) - chip) & (chips - 1)) * 2 + (peer & 1)
    ranks = bucket_ranks(slot_row, faces // WIDE, n_blocks, rank_lhs)
    send, recv, wgt = send_ref[...], recv_ref[...], wgt_ref[...]
    w_high, w_low = halves(wgt)
    recv_row = recv >> 7
    maps = slot_maps(
        slot_row,
        n_blocks,
        ranks,
        (
            (send >> 7).astype(f32),
            (send & 127).astype(f32),
            w_high,
            w_low,
            (recv_row & (half_y - 1)).astype(f32),
            (recv & 127).astype(f32),
            jnp.where(recv_row >= half_y, 128.0, 0.0),
        ),
        map_lhs,
        map_hot,
    )
    nb = n_blocks
    srow_m[...] = maps[0:nb]
    scol_m[...] = maps[nb : 2 * nb]
    wgt_m[...] = maps[2 * nb : 3 * nb] + maps[3 * nb : 4 * nb]
    sbuf0[:, fields, :] = maps[4 * nb : 5 * nb]
    sbuf0[:, fields + 1, :] = maps[5 * nb : 6 * nb] + maps[6 * nb : 7 * nb]

    def build(t, carry):
        hot = jnp.where(fiota((LANES, WIDE), 0) == pair_at(scol_m, t), 1.0, 0.0).astype(bf16)
        chot[t, 0:LANES] = hot
        chot[t, LANES:WIDE] = hot
        wmask[t] = jnp.where(fiota((rows_y, WIDE), 0) == pair_at(srow_m, t), pair_at(wgt_m, t), 0.0)
        return carry

    lax.fori_loop(0, chips, build, 0)

    def set_lam(value):
        lam[...] = value
        high, low = halves(value)
        xhl[:, 0:LANES] = high.astype(bf16)
        xhl[:, LANES:WIDE] = low.astype(bf16)

    def gathered(hot, mask):
        found = dot(xhl[...], hot).reshape(fields, rows_y, WIDE)
        return jnp.sum(found * mask[None], axis=1)

    set_lam(start_ref[...].reshape(fields * rows_y, LANES))

    def to_chip(t, k):
        return lax.rem(chip + t, chips) * 2 + k

    def send_sweep(sweep):
        sb, rb = (sbuf0, rbuf0) if sweep == 0 else (sbuf1.at[sweep - 1], rbuf1.at[sweep - 1])

        def fill(t):
            value = gathered(chot[t], wmask[t])
            sb[2 * t, 0:fields] = value[:, 0:LANES]
            sb[2 * t + 1, 0:fields] = value[:, LANES:WIDE]

        def body(t, carry):
            fill(t)
            for k in range(2):
                pltpu.make_async_remote_copy(
                    src_ref=sb.at[2 * t + k],
                    dst_ref=rb.at[2 * t + core],
                    send_sem=send_sem.at[sweep],
                    recv_sem=recv_sem.at[sweep, t // group],
                    device_id={"blocks": to_chip(t, k)},
                ).start()
            return carry

        lax.fori_loop(1, chips, body, 0)
        fill(0)
        pltpu.make_async_remote_copy(
            src_ref=sb.at[1 - core],
            dst_ref=rb.at[core],
            send_sem=send_sem.at[sweep],
            recv_sem=recv_sem.at[sweep, 0],
            device_id={"blocks": to_chip(0, 1 - core)},
        ).start()
        pltpu.make_async_copy(sb.at[core], rb.at[core], recv_sem.at[sweep, 0]).start()

    def wait_for(ref, sem):
        pltpu.make_async_copy(ref, ref, sem).wait()

    def receive(sweep):
        rb = rbuf0 if sweep == 0 else rbuf1.at[sweep - 1]
        total = jnp.zeros((2 * fields * half_y, WIDE), f32)
        for g in range(GROUPS):
            wait_for(rb.at[pl.ds(2 * group * g, 2 * group)], recv_sem.at[sweep, g])

            def place(t, carry):
                lanes = pl.ds(pl.multiple_of(t * WIDE, WIDE), WIDE)
                first, second = rb[2 * t], rb[2 * t + 1]
                where = jnp.concatenate([rbuf0[2 * t, fields:], rbuf0[2 * t + 1, fields:]], axis=1)
                if sweep == 0:
                    recv_hot[:, lanes] = jnp.where(fiota((WIDE, WIDE), 0) == where[1:2], 1.0, 0.0).astype(bf16)
                mask = fiota((half_y, WIDE), 0) == where[0:1]
                value = jnp.concatenate([first[0:fields], second[0:fields]], axis=1)
                for part, these in enumerate(halves(value)):
                    for f in range(fields):
                        at = (part * fields + f) * half_y
                        recv_lhs[at : at + half_y, lanes] = jnp.where(mask, these[f : f + 1], 0.0).astype(bf16)
                return carry

            lax.fori_loop(group * g, group * (g + 1), place, 0)
            lanes = slice(group * g * WIDE, group * (g + 1) * WIDE)
            total = total + dot_nt(recv_lhs[:, lanes], recv_hot[:, lanes])
        both = total[0 : fields * half_y] + total[fields * half_y :]
        face = []
        for f in range(fields):
            part = both[f * half_y : (f + 1) * half_y]
            face.append(jnp.concatenate([part[:, 0:LANES], part[:, LANES:WIDE]], axis=0))
        return face

    def update(face):
        rhs = [local[f] + face[f] for f in range(fields)]
        new = []
        for f in range(fields):
            acc = binv[f, 0] * rhs[0]
            for g in range(1, fields):
                acc = acc + binv[f, g] * rhs[g]
            new.append((1.0 - OMEGA) * lam[f * rows_y : (f + 1) * rows_y] + OMEGA * acc)
        set_lam(jnp.concatenate(new, axis=0))

    def local_terms():
        for f in range(fields):
            x = lam[f * rows_y : (f + 1) * rows_y]
            interior = coup[0] * shifted(x, 1, 0) + coup[1] * shifted(x, -1, 0)
            interior = interior + coup[2] * shifted(x, 1, 1) + coup[3] * shifted(x, -1, 1)
            local[f] = source[f] + interior

    pl.semaphore_wait(barrier, n_blocks - 1 + n_obj - 1)

    ends = (lax.rem(b + 1, n_blocks), lax.rem(b + n_blocks - 1, n_blocks))
    sides = (lax.rem(o + 1, n_obj), lax.rem(o + n_obj - 1, n_obj))

    def halo_copies(sweep, field):
        copies = []
        for k in range(2):
            edge = size_x - 1 if k == 0 else 0
            copies.append(
                pltpu.make_async_remote_copy(
                    src_ref=field.at[:, edge],
                    dst_ref=xrecv.at[sweep, k],
                    send_sem=halo_send.at[sweep, k],
                    recv_sem=halo_recv.at[sweep, k],
                    device_id={"blocks": ends[k]},
                )
            )
            copies.append(
                pltpu.make_async_remote_copy(
                    src_ref=ysend.at[sweep, k],
                    dst_ref=yrecv.at[sweep, k],
                    send_sem=halo_send.at[sweep, 2 + k],
                    recv_sem=halo_recv.at[sweep, 2 + k],
                    device_id={"obj": sides[k]},
                )
            )
        return copies

    def neighbours(sweep, field):
        x = field[...]
        zero = jnp.zeros((comps, 1, size_y, LANES), f32)
        low = jnp.where(b > 0, xrecv[sweep, 0][:, None], zero)
        high = jnp.where(b < n_blocks - 1, xrecv[sweep, 1][:, None], zero)
        beside = jnp.concatenate([x[:, 1:], high], axis=1) + jnp.concatenate([low, x[:, :-1]], axis=1)
        flat = x.reshape(comps * size_x * size_y, LANES)
        total = flat.shape[0]
        at = iota((comps, size_x, size_y, LANES), 2)
        before = jnp.where(o > 0, yrecv[sweep, 0], 0.0)[:, :, None]
        after = jnp.where(o < n_obj - 1, yrecv[sweep, 1], 0.0)[:, :, None]
        up = pltpu.roll(flat, total - 1, 0).reshape(x.shape)
        down = pltpu.roll(flat, 1, 0).reshape(x.shape)
        beside = beside + jnp.where(at == size_y - 1, after, up) + jnp.where(at == 0, before, down)
        sideways = shifted(flat, -1, 1) + shifted(flat, 1, 1)
        return x, beside + sideways.reshape(x.shape)

    send_sweep(0)
    loads[3].wait()
    ysend[0, 0] = mesh0[:, :, size_y - 1, :]
    ysend[0, 1] = mesh0[:, :, 0, :]
    halos0 = halo_copies(0, mesh0)
    for copy in halos0:
        copy.start()
    loads[0].wait()
    loads[1].wait()
    local_terms()
    loads[2].wait()

    def build_surface(t, carry):
        cell = pair_at(scell_ref, t)
        hot = jnp.where(iota((LANES, WIDE), 0) == (cell & 127), 1.0, 0.0).astype(bf16)
        surf_hot[t, 0:LANES] = hot
        surf_hot[t, LANES:WIDE] = hot
        surf_mask[t] = jnp.where(iota((rows_y, WIDE), 0) == (cell >> 7), 1.0, 0.0)
        return carry

    lax.fori_loop(0, surf // WIDE, build_surface, 0)
    update(receive(0))

    send_sweep(1)
    local_terms()
    owner, node = owner_ref[...], node_ref[...]
    bucket = (((owner >> 1) - chip) & (chips - 1)) * 2 + (owner & 1)
    relay_ranks = bucket_ranks(bucket, quarter // WIDE, n_blocks, rank_lhs)
    cap = LANES // 2
    side = ((owner & 1) ^ core) * cap
    relay_ranks = [rank + pair(side, g).astype(f32) for g, rank in enumerate(relay_ranks)]
    node_row = node >> 7
    half_nodes = size_x * size_y // 2
    relay_maps = slot_maps(
        bucket >> 1,
        chips,
        relay_ranks,
        (
            fiota((qrows, LANES), 0) + 1.0,
            fiota((qrows, LANES), 1),
            (node_row & (half_nodes - 1)).astype(f32),
            (node & 127).astype(f32),
            jnp.where(node_row >= half_nodes, 128.0, 0.0),
        ),
        map_lhs,
        map_hot,
    )
    rrow_m[...] = relay_maps[0:chips]
    rcol_m[...] = relay_maps[chips : 2 * chips]
    isend[:, 0, :] = relay_maps[2 * chips : 3 * chips]
    isend[:, 1, :] = relay_maps[3 * chips : 4 * chips] + relay_maps[4 * chips : 5 * chips]

    def relay_send(sb, rb, which, before):
        def post(t):
            for k in range(2):
                pltpu.make_async_remote_copy(
                    src_ref=sb.at[t],
                    dst_ref=rb.at[2 * t + core],
                    send_sem=send_sem.at[which],
                    recv_sem=recv_sem.at[which, 0],
                    device_id={"blocks": to_chip(t, k)},
                ).start()

        def body(u, carry):
            before(u)
            post(2 * u)
            post(2 * u + 1)
            return carry

        lax.fori_loop(1, chips // 2, body, 0)
        before(0)
        post(1)
        pltpu.make_async_remote_copy(
            src_ref=sb.at[0],
            dst_ref=rb.at[core],
            send_sem=send_sem.at[which],
            recv_sem=recv_sem.at[which, 0],
            device_id={"blocks": to_chip(0, 1 - core)},
        ).start()
        pltpu.make_async_copy(sb.at[0], rb.at[core], recv_sem.at[which, 0]).start()

    relay_send(isend, irecv, SWEEPS, lambda u: None)

    def build_relay(u, carry):
        hot = jnp.where(fiota((LANES, WIDE), 0) == pair_at(rcol_m, u), 1.0, 0.0).astype(bf16)
        relay_hot[u, 0:LANES] = hot
        relay_hot[u, LANES:WIDE] = hot
        relay_mask[u] = jnp.where(fiota((qrows, WIDE), 0) + 1.0 == pair_at(rrow_m, u), 1.0, 0.0)
        return carry

    lax.fori_loop(0, chips // 2, build_relay, 0)
    update(receive(1))

    send_sweep(2)
    local_terms()
    loads[4].wait()
    for copy in halos0:
        copy.wait_recv()
    coef[...] = OMEGA / (6.0 + stiff[...])
    centre, beside = neighbours(0, mesh0)
    base[...] = (1.0 - OMEGA) * centre + coef[...][None] * beside

    wait_for(irecv, recv_sem.at[SWEEPS, 0])
    mine = iota((1, LANES), 1) // cap == core

    def build_nodes(u, carry):
        lanes = pl.ds(pl.multiple_of(u * WIDE, WIDE), WIDE)
        where = jnp.concatenate(
            [jnp.where(mine, irecv[4 * u + 2 * k], irecv[4 * u + 2 * k + 1]) for k in range(2)], axis=1
        )
        inode[u] = where
        node_hot[:, lanes] = jnp.where(fiota((WIDE, WIDE), 0) == where[1:2], 1.0, 0.0).astype(bf16)
        return carry

    lax.fori_loop(0, chips // 2, build_nodes, 0)
    update(receive(2))
    flow_copy = pltpu.make_async_copy(lam, flow_hbm, out_sem.at[0])
    flow_copy.start()

    loads[5].wait()
    weight = oweight_ref[o]
    obj_copies = []
    for s in list(range(1, n_obj)) + [0]:
        q = lax.rem(o + s, n_obj)

        def surface(k, carry):
            t = q * (qrows // 2) + k
            value = gathered(surf_hot[t], surf_mask[t])
            lanes = pl.ds(pl.multiple_of(t * WIDE, WIDE), WIDE)
            part = grad[0, :, lanes] * value[0:1]
            for f in range(1, fields):
                part = part + grad[f, :, lanes] * value[f : f + 1]
            part = part * weight
            ssend[s, 2 * k] = part[:, 0:LANES]
            ssend[s, 2 * k + 1] = part[:, LANES:WIDE]
            return carry

        lax.fori_loop(0, qrows // 2, surface, 0)
        if s:
            copy = pltpu.make_async_remote_copy(
                src_ref=ssend.at[s],
                dst_ref=srecv.at[s - 1],
                send_sem=obj_send.at[s - 1],
                recv_sem=obj_recv.at[s - 1],
                device_id={"obj": q},
            )
            copy.start()
            obj_copies.append(copy)
    for copy in obj_copies:
        copy.wait_recv()
    comb[...] = ssend[0] + srecv[0] + srecv[1] + srecv[2]
    combined = jnp.concatenate([comb[:, c, :] for c in range(comps)], axis=0)
    high, low = halves(combined)
    vhl[:, 0:LANES] = high.astype(bf16)
    vhl[:, LANES:WIDE] = low.astype(bf16)

    def pick(u):
        found = dot(vhl[...], relay_hot[u]).reshape(comps, qrows, WIDE)
        value = jnp.sum(found * relay_mask[u][None], axis=1)
        vsend[2 * u] = value[:, 0:LANES]
        vsend[2 * u + 1] = value[:, LANES:WIDE]

    relay_send(vsend, vrecv, SWEEPS + 1, pick)

    wait_for(vrecv, recv_sem.at[SWEEPS + 1, 0])

    def place_nodes(u, carry):
        lanes = pl.ds(pl.multiple_of(u * WIDE, WIDE), WIDE)
        value = jnp.concatenate(
            [jnp.where(mine, vrecv[4 * u + 2 * k], vrecv[4 * u + 2 * k + 1]) for k in range(2)], axis=1
        )
        mask = fiota((half_nodes, WIDE), 0) == inode[u][0:1]
        for part, these in enumerate(halves(value)):
            for c in range(comps):
                at = (part * comps + c) * half_nodes
                node_lhs[at : at + half_nodes, lanes] = jnp.where(mask, these[c : c + 1], 0.0).astype(bf16)
        return carry

    lax.fori_loop(0, chips // 2, place_nodes, 0)
    forces = dot_nt(node_lhs[...], node_hot[...])
    forces = forces[0 : comps * half_nodes] + forces[comps * half_nodes :]
    forces = forces.reshape(comps, size_x // 2, size_y, WIDE)
    force = jnp.concatenate([forces[..., 0:LANES], forces[..., LANES:WIDE]], axis=1)

    scaled = coef[...][None] * force
    first = base[...] + scaled
    mesh1[...] = first
    ysend[1, 0] = mesh1[:, :, size_y - 1, :]
    ysend[1, 1] = mesh1[:, :, 0, :]
    halos1 = halo_copies(1, mesh1)
    for copy in halos1:
        copy.start()
    for copy in halos1:
        copy.wait_recv()
    centre, beside = neighbours(1, mesh1)
    mesh2[...] = (1.0 - OMEGA) * centre + scaled + coef[...][None] * beside
    mesh_copy = pltpu.make_async_copy(mesh2, meshout_hbm, out_sem.at[1])
    mesh_copy.start()

    for copy in halos0 + halos1 + obj_copies:
        copy.wait_send()
    wait_for(sbuf0.at[pl.ds(0, n_blocks - 1)], send_sem.at[0])
    for sweep in range(1, SWEEPS):
        wait_for(sbuf1.at[sweep - 1, pl.ds(0, n_blocks - 1)], send_sem.at[sweep])
    for sb, which in ((irecv, SWEEPS), (vrecv, SWEEPS + 1)):
        wait_for(sb.at[pl.ds(0, n_blocks - 1)], send_sem.at[which])
    flow_copy.wait()
    mesh_copy.wait()


def shards(
    n_blocks, n_obj, start, source, binv, coup, send, peer, recv, wgt, scell, grad, oweight, owner, node, mesh, stiff
):
    _, fields, rows_y, cols = start.shape
    faces, surf = send.shape[0], scell.shape[0]
    comps, size_x, size_y, _ = mesh.shape
    quarter = surf // n_obj
    qrows = quarter // LANES
    chips = n_blocks // 2
    half_nodes = size_x * size_y // 2
    vmem = pl.BlockSpec(memory_space=pltpu.VMEM)
    smem = pl.BlockSpec(memory_space=pltpu.SMEM)
    hbm = pl.BlockSpec(memory_space=pl.ANY)
    V = pltpu.VMEM
    dma = pltpu.SemaphoreType.DMA
    call = pl.pallas_call(
        functools.partial(kernel, n_blocks, n_obj, fields, rows_y, faces, surf, comps, size_x, size_y),
        out_shape=(
            jax.ShapeDtypeStruct((fields * rows_y, cols), f32),
            jax.ShapeDtypeStruct(mesh.shape, f32),
        ),
        in_specs=[vmem, hbm, hbm, hbm, vmem, vmem, vmem, vmem, vmem, hbm, smem, vmem, vmem, hbm, hbm],
        out_specs=(hbm, hbm),
        scratch_shapes=[
            V((fields, rows_y, cols), f32),
            V(binv.shape, f32),
            V(coup.shape, f32),
            V((fields, comps, surf), f32),
            V(mesh.shape, f32),
            V(stiff.shape, f32),
            V((faces // WIDE * n_blocks, 2 * WIDE), bf16),
            V((7 * n_blocks, faces), bf16),
            V((LANES, faces), bf16),
            V((n_blocks, LANES), f32),
            V((n_blocks, LANES), f32),
            V((n_blocks, LANES), f32),
            V((chips, WIDE, WIDE), bf16),
            V((chips, rows_y, WIDE), f32),
            V((surf // WIDE, WIDE, WIDE), bf16),
            V((surf // WIDE, rows_y, WIDE), f32),
            V((fields * rows_y, LANES), f32),
            V((fields * rows_y, WIDE), bf16),
            V((fields, rows_y, LANES), f32),
            V((n_blocks, fields + 2, LANES), f32),
            V((n_blocks, fields + 2, LANES), f32),
            V((SWEEPS - 1, n_blocks, fields, LANES), f32),
            V((SWEEPS - 1, n_blocks, fields, LANES), f32),
            V((WIDE, chips * WIDE), bf16),
            V((fields * rows_y, chips * WIDE), bf16),
            V((n_obj, qrows, comps, LANES), f32),
            V((n_obj - 1, qrows, comps, LANES), f32),
            V((qrows, comps, LANES), f32),
            V((comps * qrows, WIDE), bf16),
            V((chips, LANES), f32),
            V((chips, LANES), f32),
            V((chips // 2, WIDE, WIDE), bf16),
            V((chips // 2, qrows, WIDE), f32),
            V((chips, 2, LANES), f32),
            V((n_blocks, 2, LANES), f32),
            V((chips, comps, LANES), f32),
            V((n_blocks, comps, LANES), f32),
            V((WIDE, chips * LANES), bf16),
            V((2 * comps * half_nodes, chips * LANES), bf16),
            V((chips // 2, 2, WIDE), f32),
            V(mesh.shape, f32),
            V(mesh.shape, f32),
            V(mesh.shape, f32),
            V(stiff.shape, f32),
            V((2, 2, comps, size_x, LANES), f32),
            V((2, 2, comps, size_x, LANES), f32),
            V((2, 2, comps, size_y, LANES), f32),
            dma((6,)),
            dma((2,)),
            dma((1,)),
            dma((SWEEPS + 2,)),
            dma((SWEEPS + 2, GROUPS)),
            dma((n_obj - 1,)),
            dma((n_obj - 1,)),
            dma((2, 4)),
            dma((2, 4)),
        ],
        compiler_params=pltpu.CompilerParams(
            collective_id=0, has_side_effects=True, vmem_limit_bytes=56 * 1024 * 1024
        ),
    )
    flow, mesh_adjoint = call(
        start[0],
        source[0],
        binv,
        coup,
        send.reshape(-1, LANES),
        peer.reshape(-1, LANES),
        recv.reshape(-1, LANES),
        wgt.reshape(-1, LANES),
        scell.reshape(-1, LANES),
        jnp.transpose(grad, (1, 0, 2)),
        oweight,
        owner.reshape(-1, LANES),
        node.reshape(-1, LANES),
        mesh,
        stiff,
    )
    return flow.reshape(start.shape), mesh_adjoint


def solution(mesh):
    placed = (
        P("obj", None, "blocks", None),
        P("obj", None, "blocks", None),
        P(None, None, "blocks", None),
        P(None, "blocks", None),
        P("blocks"),
        P("blocks", None),
        P("blocks"),
        P("blocks"),
        P("blocks"),
        P(None, None, "blocks"),
        P(),
        P(("blocks", "obj"), None),
        P(("blocks", "obj")),
        P(None, "blocks", "obj", None),
        P("blocks", "obj", None),
    )
    return jax.shard_map(
        functools.partial(shards, mesh.shape["blocks"], mesh.shape["obj"]),
        mesh=mesh,
        in_specs=placed,
        out_specs=(P("obj", None, "blocks", None), P(None, "blocks", "obj", None)),
        check_vma=False,
    )
```

time: 784 us -> 77.6 us (0.10); the launches traced: 770 us -> 77.2 us
  other arithmetic: 353 us -> 0 us
  local copies, waits for them, and re-layouts: 227 us -> 2.31 us
  waiting for transfers between devices: 87.7 us -> 0 us
  starting transfers between devices: 86.8 us -> 0 us
  Pallas kernels: 0 us -> 74.2 us
  between operations: 15.5 us -> 0.65 us
    scatter-add x4 -> x0, other arithmetic: 183 us -> none  [the longest x3 154 us: shards(): jnp.zeros((fields, cell_count), jnp.float32).at[:, target_cell].add(arrived)]
    scatter x3 -> x0, other arithmetic: 114 us -> none  [shards(): packed = jnp.zeros((fields, block_count * face_cap), jnp.float32).at[:, f...]
    pallas_call x0 -> x1, Pallas kernels: none -> 74.2 us  [shards(): call(start[0], source[0], binv, coup, send.reshape(-1, LANES), peer.resha...]
    all_to_all x6 -> x0, starting transfers between devices: 64.6 us -> none  [the longest x3 29 us: shards(): lax.all_to_all(packed, 'blocks', split_axis=1, concat_axis=1, tiled=True)]
    slice x15 -> x0, local copies, waits for them, and re-layouts: 56.3 us -> none  [the longest x3 50.5 us: block_product(): accum_sum = matrix[row_idx, 0] * vector[0]]
    unnamed x120 -> x4, local copies, waits for them, and re-layouts: 51.5 us -> 2.31 us
    unnamed x2 -> x0, waiting for transfers between devices: 48.9 us -> none
    all_to_all x6 -> x0, waiting for transfers between devices: 37.7 us -> none  [the longest x3 27.8 us: shards(): lax.all_to_all(packed, 'blocks', split_axis=1, concat_axis=1, tiled=True)]
  transfers between devices with their start and end apart: 15 -> 0, of which waited for: 7 -> 0; matrix products, arithmetic and copies ran while one was open for 71% -> 0% of each run, Pallas kernels for 0% -> 0%
where the time goes in v1:
time: 77.6 us; the launch traced here: 77.2 us
  Pallas kernels  74.2 us (96%)
  local copies, waits for them, and re-layouts  2.31 us (3%)
    pallas_call x1, Pallas kernels, shards(): call(start[0], source[0], binv, coup, send.reshape(-1, LANES), peer.resha...  74.2 us
    unnamed x4, local copies, waits for them, and re-layouts  2.31 us

profile of v1, /device:TPU:1, one launch (start us, length us, event | category | flops | bytes accessed | tf_op | source)
XLA Modules:
  0.0 77.2 jit_solution(17032790837984265640)
XLA Ops:
  0.6 74.2 %shard_map.158 = (f32[320,128]{1,0:T(8,128)}, f32[3,4,32,128]{3,2,1,0:T(8,128)}) custom-call(f32[5,64,128]{2,1,0:T(8,128)} %bitcast.12, f32[5,64,128]{2,1,0:T(8,128)} %bitcast.13, f32[5,5,64,128]{3,2,1,0:T(8,128)} %binv_hbm.1, f32[4,64,128]{2,1,0:T(8,128)} %coup_hbm.1, s32[32,128]{1,0:T(8,128)} %bitcast.16, s32[32,128]{1,0:T(8,128)} %bitcast.17, ...), custom_call_target="tpu_custom_call" | custom-call | tf_op jit(solution)/shard_map/pallas_call | solution.py:603
  74.8 0.0 copy-start
  74.8 1.6 %copy.19 = f32[1,5,64,128]{3,2,1,0:T(8,128)} copy(f32[1,5,64,128]{3,2,1,0:T(8,128)} %bitcast.14) | data formatting | bytes 327680
  76.5 0.0 copy-done
  76.5 0.7 copy.20
Async XLA Ops:
  74.8 1.6 %copy-start = (f32[3,4,32,128]{3,2,1,0:T(8,128)S(1)}, f32[3,4,32,128]{3,2,1,0:T(8,128)}, u32[]{:S(2)}) copy-start(f32[3,4,32,128]{3,2,1,0:T(8,128)} %get-tuple-element.9) | copy-start | bytes 589828

commit v2 on v1

--- a/solution.py
+++ b/solution.py
@@ -10,6 +10,9 @@
 OMEGA = 0.8
 SWEEPS = 3
 GROUPS = 4
+BATCH = 8
+CHAIN = 4
+RING_Y = 4
 
 f32, bf16, i32 = jnp.float32, jnp.bfloat16, jnp.int32
 LANES = 128
@@ -30,6 +33,15 @@
 
 def fiota(shape, dim):
     return iota(shape, dim).astype(f32)
+
+
+def far_first(i, n):
+    return (n // 2 + (1 - 2 * (i % 2)) * ((i + 1) // 2)) % n
+
+
+def place_of(distance, n):
+    d = distance - n // 2
+    return jnp.where(d < 0, -2 * d - 1, 2 * d)
 
 
 def halves(x):
@@ -57,25 +69,29 @@
         before = before + hot
     a, b = iota((2 * WIDE, WIDE), 0), iota((2 * WIDE, WIDE), 1)
     upto = jnp.where((a <= b) | (a >= WIDE), 1.0, 0.0).astype(bf16)
-    counts = dot(lhs[0 : chunks * buckets, :], upto)
+    middle = chunks * buckets // 2
+    counts = [dot(lhs[0:middle, :], upto), dot(lhs[middle : 2 * middle, :], upto)]
     ranks = []
     for g in range(chunks):
         hot = jnp.where(ids == pair(bucket, g), 1.0, 0.0)
-        ranks.append(jnp.sum(counts[g * buckets : (g + 1) * buckets] * hot, axis=0, keepdims=True) - 1.0)
+        at = g % (chunks // 2) * buckets
+        ranks.append(jnp.sum(counts[2 * g // chunks][at : at + buckets] * hot, axis=0, keepdims=True) - 1.0)
     return ranks
 
 
-def slot_maps(row_of, rows, ranks, values, lhs, hot_slot):
+def slot_maps(row_of, rows, ranks, width, values, lhs, hot_slot):
     ids = iota((rows, WIDE), 0)
-    slots = fiota((LANES, WIDE), 0)
+    slots = fiota((width, WIDE), 0)
     chunks = len(ranks)
     for g in range(chunks):
         lanes = slice(g * WIDE, (g + 1) * WIDE)
-        hot_slot[:, lanes] = jnp.where(slots == ranks[g], 1.0, 0.0).astype(bf16)
+        hot_slot[0:width, lanes] = jnp.where(slots == ranks[g], 1.0, 0.0).astype(bf16)
         mask = ids == pair(row_of, g)
         for j, value in enumerate(values):
             lhs[j * rows : (j + 1) * rows, lanes] = jnp.where(mask, pair(value, g), 0.0).astype(bf16)
-    return dot_nt(lhs[0 : len(values) * rows, 0 : chunks * WIDE], hot_slot[:, 0 : chunks * WIDE])
+    middle, high = chunks * WIDE // 2, len(values) * rows
+    first = dot_nt(lhs[0:high, 0:middle], hot_slot[0:width, 0:middle])
+    return first + dot_nt(lhs[0:high, middle : 2 * middle], hot_slot[0:width, middle : 2 * middle])
 
 
 def shifted(x, shift, axis):
@@ -87,17 +103,17 @@
 
 def kernel(
     n_blocks, n_obj, fields, rows_y, faces, surf, comps, size_x, size_y,
-    start_ref, source_hbm, binv_hbm, coup_hbm, send_ref, peer_ref, recv_ref, wgt_ref, scell_ref, grad_hbm, oweight_ref,
-    owner_ref, node_ref, mesh_hbm, stiff_hbm,
-    flow_hbm, meshout_hbm,
-    source, binv, coup, grad, mesh0, stiff,
+    start_hbm, source_hbm, binv_hbm, coup_hbm, send_hbm, peer_hbm, recv_hbm, wgt_hbm, scell_hbm, grad_hbm, oweight_ref,
+    owner_hbm, node_hbm, mesh_hbm, stiff_hbm,
+    lam, mesh2,
+    source, binv, coup, grad, mesh0, stiff, peer_ref, send_ref, recv_ref, wgt_ref, start_ref, scell_ref, owner_ref, node_ref,
     rank_lhs, map_lhs, map_hot, scol_m, srow_m, wgt_m,
-    chot, wmask, surf_hot, surf_mask, lam, xhl, local,
+    chot, wmask, surf_hot, surf_mask, xhl, local,
     sbuf0, rbuf0, sbuf1, rbuf1, recv_hot, recv_lhs,
     ssend, srecv, comb, vhl,
-    rcol_m, rrow_m, relay_hot, relay_mask, isend, irecv, vsend, vrecv, node_hot, node_lhs, inode,
-    mesh1, mesh2, base, coef, ysend, yrecv, xrecv,
-    in_sem, out_sem, self_sem, send_sem, recv_sem, obj_send, obj_recv, halo_send, halo_recv,
+    recv_row_m, rcol_m, rrow_m, relay_hot, relay_mask, isend, irecv, vsend, vrecv, node_hot, node_lhs, inode,
+    mesh1, base, coef, ysend, yrecv, xrecv,
+    in_sem, send_sem, recv_sem, obj_send, obj_recv, halo_send, halo_recv,
 ):
     b, o = lax.axis_index("blocks"), lax.axis_index("obj")
     chips = n_blocks // 2
@@ -107,61 +123,81 @@
     quarter = surf // n_obj
     qrows = quarter // LANES
 
+    ring_z = chips // RING_Y
+    chip_z, chip_y = chip // RING_Y, chip % RING_Y
+    last = chips - 1
+
+    z_part = [lax.rem(chip_z + far_first(i, ring_z), ring_z) * (2 * RING_Y) for i in range(ring_z)]
+    y_part = [lax.rem(chip_y + far_first(i, RING_Y), RING_Y) * 2 for i in range(RING_Y)]
+
+    def to_chip(t, k):
+        return z_part[t // RING_Y] + y_part[t % RING_Y] + k
+
+    def slot_of(block):
+        z = place_of(((block // (2 * RING_Y)) - chip_z) & (ring_z - 1), ring_z)
+        y = place_of(((block // 2) - chip_y) & (RING_Y - 1), RING_Y)
+        return (z * RING_Y + y) * 2 + (block & 1)
+
     barrier = pltpu.get_barrier_semaphore()
 
-    def greet(t, carry):
-        pl.semaphore_signal(barrier, inc=1, device_id={"blocks": lax.rem(b + t, n_blocks)})
-        return carry
-
-    lax.fori_loop(1, n_blocks, greet, 0)
+    loads = []
+    for k, (src, dst) in enumerate(
+        (
+            (source_hbm, source), (coup_hbm, coup), (binv_hbm, binv), (mesh_hbm, mesh0), (stiff_hbm, stiff), (grad_hbm, grad),
+            (peer_hbm, peer_ref), (send_hbm, send_ref), (recv_hbm, recv_ref), (wgt_hbm, wgt_ref), (start_hbm, start_ref),
+            (scell_hbm, scell_ref), (owner_hbm, owner_ref), (node_hbm, node_ref),
+        )
+    ):
+        loads.append(pltpu.make_async_copy(src, dst, in_sem.at[k]))
+    for k in (*range(6, len(loads)), *range(6)):
+        loads[k].start()
+
+    for t in range(last):
+        for k in range(2):
+            pl.semaphore_signal(barrier, inc=1, device_id={"blocks": to_chip(t, k)})
+    pl.semaphore_signal(barrier, inc=1, device_id={"blocks": to_chip(last, 1 - core)})
     for s in range(1, n_obj):
         pl.semaphore_signal(barrier, inc=1, device_id={"obj": lax.rem(o + s, n_obj)})
 
-    loads = []
-    for k, (src, dst) in enumerate(
-        ((source_hbm, source), (coup_hbm, coup), (binv_hbm, binv), (mesh_hbm, mesh0), (stiff_hbm, stiff), (grad_hbm, grad))
-    ):
-        copy = pltpu.make_async_copy(src, dst, in_sem.at[k])
-        copy.start()
-        loads.append(copy)
+    for k in range(6, 10):
+        loads[k].wait()
 
     peer = peer_ref[...]
-    slot_row = (((peer >> 1) - chip) & (chips - 1)) * 2 + (peer & 1)
+    slot_row = slot_of(peer)
     ranks = bucket_ranks(slot_row, faces // WIDE, n_blocks, rank_lhs)
     send, recv, wgt = send_ref[...], recv_ref[...], wgt_ref[...]
     w_high, w_low = halves(wgt)
-    recv_row = recv >> 7
+    side = (slot_row & 1) * LANES
     maps = slot_maps(
-        slot_row,
-        n_blocks,
-        ranks,
+        slot_row >> 1,
+        chips,
+        [rank + pair(side, g).astype(f32) for g, rank in enumerate(ranks)],
+        WIDE,
         (
             (send >> 7).astype(f32),
             (send & 127).astype(f32),
             w_high,
             w_low,
-            (recv_row & (half_y - 1)).astype(f32),
+            (recv >> 7).astype(f32),
             (recv & 127).astype(f32),
-            jnp.where(recv_row >= half_y, 128.0, 0.0),
         ),
         map_lhs,
         map_hot,
     )
-    nb = n_blocks
-    srow_m[...] = maps[0:nb]
-    scol_m[...] = maps[nb : 2 * nb]
-    wgt_m[...] = maps[2 * nb : 3 * nb] + maps[3 * nb : 4 * nb]
-    sbuf0[:, fields, :] = maps[4 * nb : 5 * nb]
-    sbuf0[:, fields + 1, :] = maps[5 * nb : 6 * nb] + maps[6 * nb : 7 * nb]
+    srow_m[...] = maps[0:chips]
+    scol_m[...] = maps[chips : 2 * chips]
+    wgt_m[...] = maps[2 * chips : 3 * chips] + maps[3 * chips : 4 * chips]
+    target = maps[4 * chips : 5 * chips] * 128.0 + maps[5 * chips : 6 * chips]
+    for t in range(chips):
+        sbuf0[2 * t, fields:] = target[t : t + 1, 0:LANES]
+        sbuf0[2 * t + 1, fields:] = target[t : t + 1, LANES:WIDE]
 
     def build(t, carry):
-        hot = jnp.where(fiota((LANES, WIDE), 0) == pair_at(scol_m, t), 1.0, 0.0).astype(bf16)
+        hot = jnp.where(fiota((LANES, WIDE), 0) == scol_m[pl.ds(t, 1), :], 1.0, 0.0).astype(bf16)
         chot[t, 0:LANES] = hot
         chot[t, LANES:WIDE] = hot
-        wmask[t] = jnp.where(fiota((rows_y, WIDE), 0) == pair_at(srow_m, t), pair_at(wgt_m, t), 0.0)
+        wmask[t] = jnp.where(fiota((rows_y, WIDE), 0) == srow_m[pl.ds(t, 1), :], wgt_m[pl.ds(t, 1), :], 0.0)
         return carry
-
-    lax.fori_loop(0, chips, build, 0)
 
     def set_lam(value):
         lam[...] = value
@@ -173,68 +209,77 @@
         found = dot(xhl[...], hot).reshape(fields, rows_y, WIDE)
         return jnp.sum(found * mask[None], axis=1)
 
+    loads[10].wait()
     set_lam(start_ref[...].reshape(fields * rows_y, LANES))
-
-    def to_chip(t, k):
-        return lax.rem(chip + t, chips) * 2 + k
 
     def send_sweep(sweep):
         sb, rb = (sbuf0, rbuf0) if sweep == 0 else (sbuf1.at[sweep - 1], rbuf1.at[sweep - 1])
 
-        def fill(t):
-            value = gathered(chot[t], wmask[t])
-            sb[2 * t, 0:fields] = value[:, 0:LANES]
-            sb[2 * t + 1, 0:fields] = value[:, LANES:WIDE]
-
-        def body(t, carry):
-            fill(t)
+        def fill(first):
+            values = [gathered(chot[first + j], wmask[first + j]) for j in range(group)]
+            for j, value in enumerate(values):
+                sb[2 * (first + j), 0:fields] = value[:, 0:LANES]
+                sb[2 * (first + j) + 1, 0:fields] = value[:, LANES:WIDE]
+
+        def post(t, g):
             for k in range(2):
                 pltpu.make_async_remote_copy(
                     src_ref=sb.at[2 * t + k],
                     dst_ref=rb.at[2 * t + core],
                     send_sem=send_sem.at[sweep],
-                    recv_sem=recv_sem.at[sweep, t // group],
+                    recv_sem=recv_sem.at[sweep, g],
                     device_id={"blocks": to_chip(t, k)},
                 ).start()
-            return carry
-
-        lax.fori_loop(1, chips, body, 0)
-        fill(0)
+
+        for g in range(GROUPS):
+            if sweep == 0:
+                lax.fori_loop(group * g, group * (g + 1), build, 0)
+            fill(group * g)
+            if sweep == 0 and g == 0:
+                pl.semaphore_wait(barrier, n_blocks - 1 + n_obj - 1)
+            for t in range(group * g, min(group * (g + 1), last)):
+                post(t, g)
         pltpu.make_async_remote_copy(
-            src_ref=sb.at[1 - core],
-            dst_ref=rb.at[core],
+            src_ref=sb.at[2 * last + 1 - core],
+            dst_ref=rb.at[2 * last + core],
             send_sem=send_sem.at[sweep],
-            recv_sem=recv_sem.at[sweep, 0],
-            device_id={"blocks": to_chip(0, 1 - core)},
+            recv_sem=recv_sem.at[sweep, GROUPS - 1],
+            device_id={"blocks": to_chip(last, 1 - core)},
         ).start()
-        pltpu.make_async_copy(sb.at[core], rb.at[core], recv_sem.at[sweep, 0]).start()
+        pltpu.make_async_copy(sb.at[2 * last + core], rb.at[2 * last + core], recv_sem.at[sweep, GROUPS - 1]).start()
 
     def wait_for(ref, sem):
         pltpu.make_async_copy(ref, ref, sem).wait()
 
     def receive(sweep):
         rb = rbuf0 if sweep == 0 else rbuf1.at[sweep - 1]
-        total = jnp.zeros((2 * fields * half_y, WIDE), f32)
+        def place(t):
+            lanes = slice(t * WIDE, (t + 1) * WIDE)
+            first, second = rb[2 * t], rb[2 * t + 1]
+            if sweep == 0:
+                cell = jnp.concatenate([first[fields:], second[fields:]], axis=1).astype(i32)
+                row = cell >> 7
+                col = (cell & 127) + jnp.where(row >= half_y, LANES, 0)
+                recv_row_m[t] = row & (half_y - 1)
+                recv_hot[:, lanes] = jnp.where(iota((WIDE, WIDE), 0) == col, 1.0, 0.0).astype(bf16)
+            mask = iota((half_y, WIDE), 0) == recv_row_m[t]
+            value = jnp.concatenate([first[0:fields], second[0:fields]], axis=1)
+            for part, these in enumerate(halves(value)):
+                for f in range(fields):
+                    at = (part * fields + f) * half_y
+                    recv_lhs[at : at + half_y, lanes] = jnp.where(mask, these[f : f + 1], 0.0).astype(bf16)
+
+        total = None
         for g in range(GROUPS):
             wait_for(rb.at[pl.ds(2 * group * g, 2 * group)], recv_sem.at[sweep, g])
-
-            def place(t, carry):
-                lanes = pl.ds(pl.multiple_of(t * WIDE, WIDE), WIDE)
-                first, second = rb[2 * t], rb[2 * t + 1]
-                where = jnp.concatenate([rbuf0[2 * t, fields:], rbuf0[2 * t + 1, fields:]], axis=1)
-                if sweep == 0:
-                    recv_hot[:, lanes] = jnp.where(fiota((WIDE, WIDE), 0) == where[1:2], 1.0, 0.0).astype(bf16)
-                mask = fiota((half_y, WIDE), 0) == where[0:1]
-                value = jnp.concatenate([first[0:fields], second[0:fields]], axis=1)
-                for part, these in enumerate(halves(value)):
-                    for f in range(fields):
-                        at = (part * fields + f) * half_y
-                        recv_lhs[at : at + half_y, lanes] = jnp.where(mask, these[f : f + 1], 0.0).astype(bf16)
-                return carry
-
-            lax.fori_loop(group * g, group * (g + 1), place, 0)
-            lanes = slice(group * g * WIDE, group * (g + 1) * WIDE)
-            total = total + dot_nt(recv_lhs[:, lanes], recv_hot[:, lanes])
+            if g % 2 == 0:
+                continue
+            for t in range((g - 1) * group, (g + 1) * group, CHAIN):
+                for j in range(CHAIN):
+                    place(t + j)
+                lanes = slice(t * WIDE, (t + CHAIN) * WIDE)
+                part = dot_nt(recv_lhs[:, lanes], recv_hot[:, lanes])
+                total = part if total is None else total + part
         both = total[0 : fields * half_y] + total[fields * half_y :]
         face = []
         for f in range(fields):
@@ -258,8 +303,6 @@
             interior = coup[0] * shifted(x, 1, 0) + coup[1] * shifted(x, -1, 0)
             interior = interior + coup[2] * shifted(x, 1, 1) + coup[3] * shifted(x, -1, 1)
             local[f] = source[f] + interior
-
-    pl.semaphore_wait(barrier, n_blocks - 1 + n_obj - 1)
 
     ends = (lax.rem(b + 1, n_blocks), lax.rem(b + n_blocks - 1, n_blocks))
     sides = (lax.rem(o + 1, n_obj), lax.rem(o + n_obj - 1, n_obj))
@@ -325,13 +368,16 @@
         surf_mask[t] = jnp.where(iota((rows_y, WIDE), 0) == (cell >> 7), 1.0, 0.0)
         return carry
 
+    loads[11].wait()
     lax.fori_loop(0, surf // WIDE, build_surface, 0)
     update(receive(0))
 
     send_sweep(1)
     local_terms()
+    loads[12].wait()
+    loads[13].wait()
     owner, node = owner_ref[...], node_ref[...]
-    bucket = (((owner >> 1) - chip) & (chips - 1)) * 2 + (owner & 1)
+    bucket = slot_of(owner)
     relay_ranks = bucket_ranks(bucket, quarter // WIDE, n_blocks, rank_lhs)
     cap = LANES // 2
     side = ((owner & 1) ^ core) * cap
@@ -342,6 +388,7 @@
         bucket >> 1,
         chips,
         relay_ranks,
+        LANES,
         (
             fiota((qrows, LANES), 0) + 1.0,
             fiota((qrows, LANES), 1),
@@ -368,23 +415,20 @@
                     device_id={"blocks": to_chip(t, k)},
                 ).start()
 
-        def body(u, carry):
-            before(u)
-            post(2 * u)
-            post(2 * u + 1)
-            return carry
-
-        lax.fori_loop(1, chips // 2, body, 0)
         before(0)
-        post(1)
+        for t in range(2 * BATCH):
+            post(t)
+        before(BATCH)
+        for t in range(2 * BATCH, last):
+            post(t)
         pltpu.make_async_remote_copy(
-            src_ref=sb.at[0],
-            dst_ref=rb.at[core],
+            src_ref=sb.at[last],
+            dst_ref=rb.at[2 * last + core],
             send_sem=send_sem.at[which],
             recv_sem=recv_sem.at[which, 0],
-            device_id={"blocks": to_chip(0, 1 - core)},
+            device_id={"blocks": to_chip(last, 1 - core)},
         ).start()
-        pltpu.make_async_copy(sb.at[0], rb.at[core], recv_sem.at[which, 0]).start()
+        pltpu.make_async_copy(sb.at[last], rb.at[2 * last + core], recv_sem.at[which, 0]).start()
 
     relay_send(isend, irecv, SWEEPS, lambda u: None)
 
@@ -421,28 +465,23 @@
 
     lax.fori_loop(0, chips // 2, build_nodes, 0)
     update(receive(2))
-    flow_copy = pltpu.make_async_copy(lam, flow_hbm, out_sem.at[0])
-    flow_copy.start()
 
     loads[5].wait()
     weight = oweight_ref[o]
     obj_copies = []
-    for s in list(range(1, n_obj)) + [0]:
+    for s in [n_obj // 2, *(s for s in range(1, n_obj) if s != n_obj // 2), 0]:
         q = lax.rem(o + s, n_obj)
 
-        def surface(k, carry):
-            t = q * (qrows // 2) + k
-            value = gathered(surf_hot[t], surf_mask[t])
-            lanes = pl.ds(pl.multiple_of(t * WIDE, WIDE), WIDE)
+        first = q * (qrows // 2)
+        values = [gathered(surf_hot[first + k], surf_mask[first + k]) for k in range(qrows // 2)]
+        for k, value in enumerate(values):
+            lanes = pl.ds(pl.multiple_of((first + k) * WIDE, WIDE), WIDE)
             part = grad[0, :, lanes] * value[0:1]
             for f in range(1, fields):
                 part = part + grad[f, :, lanes] * value[f : f + 1]
             part = part * weight
             ssend[s, 2 * k] = part[:, 0:LANES]
             ssend[s, 2 * k + 1] = part[:, LANES:WIDE]
-            return carry
-
-        lax.fori_loop(0, qrows // 2, surface, 0)
         if s:
             copy = pltpu.make_async_remote_copy(
                 src_ref=ssend.at[s],
@@ -461,18 +500,21 @@
     vhl[:, 0:LANES] = high.astype(bf16)
     vhl[:, LANES:WIDE] = low.astype(bf16)
 
-    def pick(u):
-        found = dot(vhl[...], relay_hot[u]).reshape(comps, qrows, WIDE)
-        value = jnp.sum(found * relay_mask[u][None], axis=1)
-        vsend[2 * u] = value[:, 0:LANES]
-        vsend[2 * u + 1] = value[:, LANES:WIDE]
+    def pick(first):
+        values = []
+        for u in range(first, first + BATCH):
+            found = dot(vhl[...], relay_hot[u]).reshape(comps, qrows, WIDE)
+            values.append(jnp.sum(found * relay_mask[u][None], axis=1))
+        for u, value in enumerate(values, first):
+            vsend[2 * u] = value[:, 0:LANES]
+            vsend[2 * u + 1] = value[:, LANES:WIDE]
 
     relay_send(vsend, vrecv, SWEEPS + 1, pick)
 
     wait_for(vrecv, recv_sem.at[SWEEPS + 1, 0])
 
-    def place_nodes(u, carry):
-        lanes = pl.ds(pl.multiple_of(u * WIDE, WIDE), WIDE)
+    def place_nodes(u):
+        lanes = slice(u * WIDE, (u + 1) * WIDE)
         value = jnp.concatenate(
             [jnp.where(mine, vrecv[4 * u + 2 * k], vrecv[4 * u + 2 * k + 1]) for k in range(2)], axis=1
         )
@@ -481,10 +523,14 @@
             for c in range(comps):
                 at = (part * comps + c) * half_nodes
                 node_lhs[at : at + half_nodes, lanes] = jnp.where(mask, these[c : c + 1], 0.0).astype(bf16)
-        return carry
-
-    lax.fori_loop(0, chips // 2, place_nodes, 0)
-    forces = dot_nt(node_lhs[...], node_hot[...])
+
+    forces = None
+    for u in range(0, chips // 2, CHAIN):
+        for j in range(CHAIN):
+            place_nodes(u + j)
+        lanes = slice(u * WIDE, (u + CHAIN) * WIDE)
+        part = dot_nt(node_lhs[:, lanes], node_hot[:, lanes])
+        forces = part if forces is None else forces + part
     forces = forces[0 : comps * half_nodes] + forces[comps * half_nodes :]
     forces = forces.reshape(comps, size_x // 2, size_y, WIDE)
     force = jnp.concatenate([forces[..., 0:LANES], forces[..., LANES:WIDE]], axis=1)
@@ -501,8 +547,6 @@
         copy.wait_recv()
     centre, beside = neighbours(1, mesh1)
     mesh2[...] = (1.0 - OMEGA) * centre + scaled + coef[...][None] * beside
-    mesh_copy = pltpu.make_async_copy(mesh2, meshout_hbm, out_sem.at[1])
-    mesh_copy.start()
 
     for copy in halos0 + halos1 + obj_copies:
         copy.wait_send()
@@ -511,8 +555,6 @@
         wait_for(sbuf1.at[sweep - 1, pl.ds(0, n_blocks - 1)], send_sem.at[sweep])
     for sb, which in ((irecv, SWEEPS), (vrecv, SWEEPS + 1)):
         wait_for(sb.at[pl.ds(0, n_blocks - 1)], send_sem.at[which])
-    flow_copy.wait()
-    mesh_copy.wait()
 
 
 def shards(
@@ -533,11 +575,11 @@
     call = pl.pallas_call(
         functools.partial(kernel, n_blocks, n_obj, fields, rows_y, faces, surf, comps, size_x, size_y),
         out_shape=(
-            jax.ShapeDtypeStruct((fields * rows_y, cols), f32),
-            jax.ShapeDtypeStruct(mesh.shape, f32),
+            V((fields * rows_y, cols), f32),
+            V(mesh.shape, f32),
         ),
-        in_specs=[vmem, hbm, hbm, hbm, vmem, vmem, vmem, vmem, vmem, hbm, smem, vmem, vmem, hbm, hbm],
-        out_specs=(hbm, hbm),
+        in_specs=[hbm] * 10 + [smem] + [hbm] * 4,
+        out_specs=(vmem, vmem),
         scratch_shapes=[
             V((fields, rows_y, cols), f32),
             V(binv.shape, f32),
@@ -545,21 +587,28 @@
             V((fields, comps, surf), f32),
             V(mesh.shape, f32),
             V(stiff.shape, f32),
+            V((faces // LANES, LANES), i32),
+            V((faces // LANES, LANES), i32),
+            V((faces // LANES, LANES), i32),
+            V((faces // LANES, LANES), f32),
+            V((fields, rows_y, cols), f32),
+            V((surf // LANES, LANES), i32),
+            V((qrows, LANES), i32),
+            V((qrows, LANES), i32),
             V((faces // WIDE * n_blocks, 2 * WIDE), bf16),
-            V((7 * n_blocks, faces), bf16),
-            V((LANES, faces), bf16),
-            V((n_blocks, LANES), f32),
-            V((n_blocks, LANES), f32),
-            V((n_blocks, LANES), f32),
+            V((6 * chips, faces), bf16),
+            V((WIDE, faces), bf16),
+            V((chips, WIDE), f32),
+            V((chips, WIDE), f32),
+            V((chips, WIDE), f32),
             V((chips, WIDE, WIDE), bf16),
             V((chips, rows_y, WIDE), f32),
             V((surf // WIDE, WIDE, WIDE), bf16),
             V((surf // WIDE, rows_y, WIDE), f32),
-            V((fields * rows_y, LANES), f32),
             V((fields * rows_y, WIDE), bf16),
             V((fields, rows_y, LANES), f32),
-            V((n_blocks, fields + 2, LANES), f32),
-            V((n_blocks, fields + 2, LANES), f32),
+            V((n_blocks, fields + 1, LANES), f32),
+            V((n_blocks, fields + 1, LANES), f32),
             V((SWEEPS - 1, n_blocks, fields, LANES), f32),
             V((SWEEPS - 1, n_blocks, fields, LANES), f32),
             V((WIDE, chips * WIDE), bf16),
@@ -568,6 +617,7 @@
             V((n_obj - 1, qrows, comps, LANES), f32),
             V((qrows, comps, LANES), f32),
             V((comps * qrows, WIDE), bf16),
+            V((chips, 1, WIDE), i32),
             V((chips, LANES), f32),
             V((chips, LANES), f32),
             V((chips // 2, WIDE, WIDE), bf16),
@@ -581,14 +631,11 @@
             V((chips // 2, 2, WIDE), f32),
             V(mesh.shape, f32),
             V(mesh.shape, f32),
-            V(mesh.shape, f32),
             V(stiff.shape, f32),
             V((2, 2, comps, size_x, LANES), f32),
             V((2, 2, comps, size_x, LANES), f32),
             V((2, 2, comps, size_y, LANES), f32),
-            dma((6,)),
-            dma((2,)),
-            dma((1,)),
+            dma((14,)),
             dma((SWEEPS + 2,)),
             dma((SWEEPS + 2, GROUPS)),
             dma((n_obj - 1,)),

time: 77.6 us -> 64 us (0.82)
  Pallas kernels: 74.2 us -> 61.8 us
  local copies, waits for them, and re-layouts: 2.31 us -> 1.35 us
    pallas_call x1, Pallas kernels: 74.2 us -> 61.8 us  [shards(): call(start[0], source[0], binv, coup, send.reshape(-1, LANES), peer.resha...]
    unnamed x4 -> x2, local copies, waits for them, and re-layouts: 2.31 us -> 1.35 us
where the time goes in v2:
time: 64 us; the launch traced here: 63.8 us
  Pallas kernels  61.8 us (97%)
  local copies, waits for them, and re-layouts  1.35 us (2%)
  between operations  0.65 us (1%)
    pallas_call x1, Pallas kernels, shards(): call(start[0], source[0], binv, coup, send.reshape(-1, LANES), peer.resha...  61.8 us
    unnamed x2, local copies, waits for them, and re-layouts  1.35 us

profile of v2, /device:TPU:1, one launch (start us, length us, event | category | flops | bytes accessed | tf_op | source)
XLA Modules:
  0.0 63.8 jit_solution(559876511008377693)
XLA Ops:
  0.6 61.8 %shard_map.158 = (f32[320,128]{1,0:T(8,128)S(1)}, f32[3,4,32,128]{3,2,1,0:T(8,128)S(1)}) custom-call(f32[5,64,128]{2,1,0:T(8,128)} %bitcast.13, f32[5,64,128]{2,1,0:T(8,128)} %bitcast.14, f32[5,5,64,128]{3,2,1,0:T(8,128)} %binv_hbm.1, f32[4,64,128]{2,1,0:T(8,128)} %coup_hbm.1, s32[32,128]{1,0:T(8,128)} %bitcast.16, s32[32,128]{1,0:T(8,128)} %bitcast.17, ...), custom_call_target="tpu_custom_call" | custom-call | tf_op jit(solution)/shard_map/pallas_call | solution.py:650
  62.4 0.7 %copy.19 = f32[1,5,64,128]{3,2,1,0:T(8,128)} copy(f32[1,5,64,128]{3,2,1,0:T(8,128)S(1)} %bitcast.11) | data formatting | bytes 327680
  63.1 0.7 %copy.20 = f32[3,4,32,128]{3,2,1,0:T(8,128)} copy(f32[3,4,32,128]{3,2,1,0:T(8,128)S(1)} %get-tuple-element.7) | data formatting | bytes 393216

commit v3 on v2

--- a/solution.py
+++ b/solution.py
@@ -13,6 +13,8 @@
 BATCH = 8
 CHAIN = 4
 RING_Y = 4
+POSTS = (0, 4, 8, 16, 24, 32)
+TAKEN = ((0, 1), (2, 3))
 
 f32, bf16, i32 = jnp.float32, jnp.bfloat16, jnp.int32
 LANES = 128
@@ -60,38 +62,39 @@
 def bucket_ranks(bucket, chunks, buckets, lhs):
     before = jnp.zeros((buckets, WIDE), f32)
     ids = iota((buckets, WIDE), 0)
-    hots = []
-    for g in range(chunks):
-        hot = jnp.where(ids == pair(bucket, g), 1.0, 0.0)
-        rows = slice(g * buckets, (g + 1) * buckets)
-        lhs[rows, 0:WIDE] = hot.astype(bf16)
-        lhs[rows, WIDE : 2 * WIDE] = before.astype(bf16)
-        before = before + hot
     a, b = iota((2 * WIDE, WIDE), 0), iota((2 * WIDE, WIDE), 1)
     upto = jnp.where((a <= b) | (a >= WIDE), 1.0, 0.0).astype(bf16)
-    middle = chunks * buckets // 2
-    counts = [dot(lhs[0:middle, :], upto), dot(lhs[middle : 2 * middle, :], upto)]
     ranks = []
-    for g in range(chunks):
-        hot = jnp.where(ids == pair(bucket, g), 1.0, 0.0)
-        at = g % (chunks // 2) * buckets
-        ranks.append(jnp.sum(counts[2 * g // chunks][at : at + buckets] * hot, axis=0, keepdims=True) - 1.0)
+    for c in range(0, chunks, CHAIN):
+        hots = []
+        for g in range(c, c + CHAIN):
+            hot = jnp.where(ids == pair(bucket, g), 1.0, 0.0)
+            rows = slice(g * buckets, (g + 1) * buckets)
+            lhs[rows, 0:WIDE] = hot.astype(bf16)
+            lhs[rows, WIDE : 2 * WIDE] = before.astype(bf16)
+            before = before + hot
+            hots.append(hot)
+        counts = dot(lhs[c * buckets : (c + CHAIN) * buckets, :], upto)
+        for j, hot in enumerate(hots):
+            ranks.append(jnp.sum(counts[j * buckets : (j + 1) * buckets] * hot, axis=0, keepdims=True) - 1.0)
     return ranks
 
 
 def slot_maps(row_of, rows, ranks, width, values, lhs, hot_slot):
     ids = iota((rows, WIDE), 0)
     slots = fiota((width, WIDE), 0)
-    chunks = len(ranks)
-    for g in range(chunks):
-        lanes = slice(g * WIDE, (g + 1) * WIDE)
-        hot_slot[0:width, lanes] = jnp.where(slots == ranks[g], 1.0, 0.0).astype(bf16)
-        mask = ids == pair(row_of, g)
-        for j, value in enumerate(values):
-            lhs[j * rows : (j + 1) * rows, lanes] = jnp.where(mask, pair(value, g), 0.0).astype(bf16)
-    middle, high = chunks * WIDE // 2, len(values) * rows
-    first = dot_nt(lhs[0:high, 0:middle], hot_slot[0:width, 0:middle])
-    return first + dot_nt(lhs[0:high, middle : 2 * middle], hot_slot[0:width, middle : 2 * middle])
+    high, total = len(values) * rows, None
+    for c in range(0, len(ranks), CHAIN):
+        for g in range(c, c + CHAIN):
+            lanes = slice(g * WIDE, (g + 1) * WIDE)
+            hot_slot[0:width, lanes] = jnp.where(slots == ranks[g], 1.0, 0.0).astype(bf16)
+            mask = ids == pair(row_of, g)
+            for j, value in enumerate(values):
+                lhs[j * rows : (j + 1) * rows, lanes] = jnp.where(mask, pair(value, g), 0.0).astype(bf16)
+        lanes = slice(c * WIDE, (c + CHAIN) * WIDE)
+        part = dot_nt(lhs[0:high, lanes], hot_slot[0:width, lanes])
+        total = part if total is None else total + part
+    return total
 
 
 def shifted(x, shift, axis):
@@ -139,6 +142,12 @@
         return (z * RING_Y + y) * 2 + (block & 1)
 
     barrier = pltpu.get_barrier_semaphore()
+    for t in range(last):
+        for k in range(2):
+            pl.semaphore_signal(barrier, inc=1, device_id={"blocks": to_chip(t, k)})
+    pl.semaphore_signal(barrier, inc=1, device_id={"blocks": to_chip(last, 1 - core)})
+    for s in range(1, n_obj):
+        pl.semaphore_signal(barrier, inc=1, device_id={"obj": lax.rem(o + s, n_obj)})
 
     loads = []
     for k, (src, dst) in enumerate(
@@ -152,12 +161,6 @@
     for k in (*range(6, len(loads)), *range(6)):
         loads[k].start()
 
-    for t in range(last):
-        for k in range(2):
-            pl.semaphore_signal(barrier, inc=1, device_id={"blocks": to_chip(t, k)})
-    pl.semaphore_signal(barrier, inc=1, device_id={"blocks": to_chip(last, 1 - core)})
-    for s in range(1, n_obj):
-        pl.semaphore_signal(barrier, inc=1, device_id={"obj": lax.rem(o + s, n_obj)})
 
     for k in range(6, 10):
         loads[k].wait()
@@ -215,14 +218,16 @@
     def send_sweep(sweep):
         sb, rb = (sbuf0, rbuf0) if sweep == 0 else (sbuf1.at[sweep - 1], rbuf1.at[sweep - 1])
 
-        def fill(first):
-            values = [gathered(chot[first + j], wmask[first + j]) for j in range(group)]
+        def fill(first, count):
+            values = [gathered(chot[first + j], wmask[first + j]) for j in range(count)]
             for j, value in enumerate(values):
                 sb[2 * (first + j), 0:fields] = value[:, 0:LANES]
                 sb[2 * (first + j) + 1, 0:fields] = value[:, LANES:WIDE]
 
         def post(t, g):
-            for k in range(2):
+            if t == last:
+                pltpu.make_async_copy(sb.at[2 * t + core], rb.at[2 * t + core], recv_sem.at[sweep, g]).start()
+            for k in [1 - core] if t == last else range(2):
                 pltpu.make_async_remote_copy(
                     src_ref=sb.at[2 * t + k],
                     dst_ref=rb.at[2 * t + core],
@@ -231,22 +236,14 @@
                     device_id={"blocks": to_chip(t, k)},
                 ).start()
 
-        for g in range(GROUPS):
+        for first, end in zip(POSTS, POSTS[1:]):
             if sweep == 0:
-                lax.fori_loop(group * g, group * (g + 1), build, 0)
-            fill(group * g)
-            if sweep == 0 and g == 0:
+                lax.fori_loop(first, end, build, 0)
+            fill(first, end - first)
+            if sweep == 0 and first == 0:
                 pl.semaphore_wait(barrier, n_blocks - 1 + n_obj - 1)
-            for t in range(group * g, min(group * (g + 1), last)):
-                post(t, g)
-        pltpu.make_async_remote_copy(
-            src_ref=sb.at[2 * last + 1 - core],
-            dst_ref=rb.at[2 * last + core],
-            send_sem=send_sem.at[sweep],
-            recv_sem=recv_sem.at[sweep, GROUPS - 1],
-            device_id={"blocks": to_chip(last, 1 - core)},
-        ).start()
-        pltpu.make_async_copy(sb.at[2 * last + core], rb.at[2 * last + core], recv_sem.at[sweep, GROUPS - 1]).start()
+            for t in range(first, end):
+                post(t, t // group)
 
     def wait_for(ref, sem):
         pltpu.make_async_copy(ref, ref, sem).wait()
@@ -269,17 +266,18 @@
                     at = (part * fields + f) * half_y
                     recv_lhs[at : at + half_y, lanes] = jnp.where(mask, these[f : f + 1], 0.0).astype(bf16)
 
-        total = None
-        for g in range(GROUPS):
-            wait_for(rb.at[pl.ds(2 * group * g, 2 * group)], recv_sem.at[sweep, g])
-            if g % 2 == 0:
-                continue
-            for t in range((g - 1) * group, (g + 1) * group, CHAIN):
+        totals = [None, None]
+        for groups in TAKEN:
+            for g in groups:
+                wait_for(rb.at[pl.ds(2 * group * g, 2 * group)], recv_sem.at[sweep, g])
+            tiles = [t for g in groups for t in range(group * g, group * (g + 1), CHAIN)]
+            for i, t in enumerate(tiles):
                 for j in range(CHAIN):
                     place(t + j)
                 lanes = slice(t * WIDE, (t + CHAIN) * WIDE)
                 part = dot_nt(recv_lhs[:, lanes], recv_hot[:, lanes])
-                total = part if total is None else total + part
+                totals[i % 2] = part if totals[i % 2] is None else totals[i % 2] + part
+        total = totals[0] + totals[1]
         both = total[0 : fields * half_y] + total[fields * half_y :]
         face = []
         for f in range(fields):
@@ -411,7 +409,7 @@
                     src_ref=sb.at[t],
                     dst_ref=rb.at[2 * t + core],
                     send_sem=send_sem.at[which],
-                    recv_sem=recv_sem.at[which, 0],
+                    recv_sem=recv_sem.at[which, 2 * t // chips],
                     device_id={"blocks": to_chip(t, k)},
                 ).start()
 
@@ -425,10 +423,10 @@
             src_ref=sb.at[last],
             dst_ref=rb.at[2 * last + core],
             send_sem=send_sem.at[which],
-            recv_sem=recv_sem.at[which, 0],
+            recv_sem=recv_sem.at[which, 1],
             device_id={"blocks": to_chip(last, 1 - core)},
         ).start()
-        pltpu.make_async_copy(sb.at[last], rb.at[2 * last + core], recv_sem.at[which, 0]).start()
+        pltpu.make_async_copy(sb.at[last], rb.at[2 * last + core], recv_sem.at[which, 1]).start()
 
     relay_send(isend, irecv, SWEEPS, lambda u: None)
 
@@ -451,7 +449,8 @@
     centre, beside = neighbours(0, mesh0)
     base[...] = (1.0 - OMEGA) * centre + coef[...][None] * beside
 
-    wait_for(irecv, recv_sem.at[SWEEPS, 0])
+    for h in range(2):
+        wait_for(irecv.at[pl.ds(h * chips, chips)], recv_sem.at[SWEEPS, h])
     mine = iota((1, LANES), 1) // cap == core
 
     def build_nodes(u, carry):
@@ -511,8 +510,6 @@
 
     relay_send(vsend, vrecv, SWEEPS + 1, pick)
 
-    wait_for(vrecv, recv_sem.at[SWEEPS + 1, 0])
-
     def place_nodes(u):
         lanes = slice(u * WIDE, (u + 1) * WIDE)
         value = jnp.concatenate(
@@ -525,12 +522,14 @@
                 node_lhs[at : at + half_nodes, lanes] = jnp.where(mask, these[c : c + 1], 0.0).astype(bf16)
 
     forces = None
-    for u in range(0, chips // 2, CHAIN):
-        for j in range(CHAIN):
-            place_nodes(u + j)
-        lanes = slice(u * WIDE, (u + CHAIN) * WIDE)
-        part = dot_nt(node_lhs[:, lanes], node_hot[:, lanes])
-        forces = part if forces is None else forces + part
+    for h in (1, 0):
+        wait_for(vrecv.at[pl.ds(h * chips, chips)], recv_sem.at[SWEEPS + 1, h])
+        for u in range(h * chips // 4, (h + 1) * chips // 4, CHAIN):
+            for j in range(CHAIN):
+                place_nodes(u + j)
+            lanes = slice(u * WIDE, (u + CHAIN) * WIDE)
+            part = dot_nt(node_lhs[:, lanes], node_hot[:, lanes])
+            forces = part if forces is None else forces + part
     forces = forces[0 : comps * half_nodes] + forces[comps * half_nodes :]
     forces = forces.reshape(comps, size_x // 2, size_y, WIDE)
     force = jnp.concatenate([forces[..., 0:LANES], forces[..., LANES:WIDE]], axis=1)
@@ -555,6 +554,14 @@
         wait_for(sbuf1.at[sweep - 1, pl.ds(0, n_blocks - 1)], send_sem.at[sweep])
     for sb, which in ((irecv, SWEEPS), (vrecv, SWEEPS + 1)):
         wait_for(sb.at[pl.ds(0, n_blocks - 1)], send_sem.at[which])
+
+
+def write_out(flow, mesh, flow_out, mesh_out, sems):
+    copies = [pltpu.make_async_copy(flow, flow_out, sems.at[0]), pltpu.make_async_copy(mesh, mesh_out, sems.at[1])]
+    for copy in copies:
+        copy.start()
+    for copy in copies:
+        copy.wait()
 
 
 def shards(
@@ -664,6 +671,16 @@
         mesh,
         stiff,
     )
+    flow, mesh_adjoint = pl.pallas_call(
+        write_out,
+        out_shape=(jax.ShapeDtypeStruct(flow.shape, f32), jax.ShapeDtypeStruct(mesh.shape, f32)),
+        in_specs=[vmem, vmem],
+        out_specs=(hbm, hbm),
+        scratch_shapes=[dma((2,))],
+    )(
+        pltpu.with_memory_space_constraint(flow, pltpu.VMEM),
+        pltpu.with_memory_space_constraint(mesh_adjoint, pltpu.VMEM),
+    )
     return flow.reshape(start.shape), mesh_adjoint
 
 

time: 64 us -> 63.3 us (0.989)
  local copies, waits for them, and re-layouts: 1.35 us -> 0 us
    unnamed x2 -> x0, local copies, waits for them, and re-layouts: 1.35 us -> none
    pallas_call x0 -> x1, Pallas kernels: none -> 0.75 us  [shards(): pl.pallas_call(write_out, out_shape=(jax.ShapeDtypeStruct(flow.shape, f32...]
where the time goes in v3:
time: 63.3 us; the launch traced here: 63.2 us
  Pallas kernels  62.4 us (99%)
  between operations  0.8 us (1%)
    pallas_call x1, Pallas kernels, shards(): call(start[0], source[0], binv, coup, send.reshape(-1, LANES), peer.resha...  61.6 us

profile of v3, /device:TPU:1, one launch (start us, length us, event | category | flops | bytes accessed | tf_op | source)
XLA Modules:
  0.0 63.2 jit_solution(2030939153183153993)
XLA Ops:
  0.6 61.6 %shard_map.158 = (f32[320,128]{1,0:T(8,128)S(1)}, f32[3,4,32,128]{3,2,1,0:T(8,128)S(1)}) custom-call(f32[5,64,128]{2,1,0:T(8,128)} %bitcast.12, f32[5,64,128]{2,1,0:T(8,128)} %bitcast.13, f32[5,5,64,128]{3,2,1,0:T(8,128)} %binv_hbm.1, f32[4,64,128]{2,1,0:T(8,128)} %coup_hbm.1, s32[32,128]{1,0:T(8,128)} %bitcast.15, s32[32,128]{1,0:T(8,128)} %bitcast.16, ...), custom_call_target="tpu_custom_call" | custom-call | tf_op jit(solution)/shard_map/pallas_call | solution.py:657
  62.3 0.8 %shard_map.159 = (f32[320,128]{1,0:T(8,128)}, f32[3,4,32,128]{3,2,1,0:T(8,128)}) custom-call(f32[320,128]{1,0:T(8,128)S(1)} %get-tuple-element.6.flow, f32[3,4,32,128]{3,2,1,0:T(8,128)S(1)} %get-tuple-element.7.mesh), custom_call_target="tpu_custom_call" | custom-call | tf_op jit(solution)/shard_map/pallas_call | solution.py:674

commit v4 on v3

--- a/solution.py
+++ b/solution.py
@@ -11,7 +11,7 @@
 SWEEPS = 3
 GROUPS = 4
 BATCH = 8
-CHAIN = 4
+CHAIN = 2
 RING_Y = 4
 POSTS = (0, 4, 8, 16, 24, 32)
 TAKEN = ((0, 1), (2, 3))

time: 63.3 us -> 63.4 us (level)
  no operation moved by 1% of the time
where the time goes in v4:
time: 63.4 us; the launch traced here: 63.2 us
  Pallas kernels  62.4 us (98%)
  between operations  0.8 us (1%)
    pallas_call x1, Pallas kernels, shards(): call(start[0], source[0], binv, coup, send.reshape(-1, LANES), peer.resha...  61.7 us

profile of v4, /device:TPU:1, one launch (start us, length us, event | category | flops | bytes accessed | tf_op | source)
XLA Modules:
  0.0 63.2 jit_solution(13586174911686901933)
XLA Ops:
  0.6 61.7 %shard_map.158 = (f32[320,128]{1,0:T(8,128)S(1)}, f32[3,4,32,128]{3,2,1,0:T(8,128)S(1)}) custom-call(f32[5,64,128]{2,1,0:T(8,128)} %bitcast.12, f32[5,64,128]{2,1,0:T(8,128)} %bitcast.13, f32[5,5,64,128]{3,2,1,0:T(8,128)} %binv_hbm.1, f32[4,64,128]{2,1,0:T(8,128)} %coup_hbm.1, s32[32,128]{1,0:T(8,128)} %bitcast.15, s32[32,128]{1,0:T(8,128)} %bitcast.16, ...), custom_call_target="tpu_custom_call" | custom-call | tf_op jit(solution)/shard_map/pallas_call | solution.py:657
  62.3 0.8 %shard_map.159 = (f32[320,128]{1,0:T(8,128)}, f32[3,4,32,128]{3,2,1,0:T(8,128)}) custom-call(f32[320,128]{1,0:T(8,128)S(1)} %get-tuple-element.6.flow, f32[3,4,32,128]{3,2,1,0:T(8,128)S(1)} %get-tuple-element.7.mesh), custom_call_target="tpu_custom_call" | custom-call | tf_op jit(solution)/shard_map/pallas_call | solution.py:674
